TPU v7x, 128 devices: a whole 4x4x4 slice. The times are simulated.
128 devices in a mesh: tm: 32 (over x, z, y_lo), cell: 4 (over y_hi, core).
Axes of the slice: x: 4, y: 4 (y_hi: 2, y_lo: 2; y = y_hi * 2 + y_lo), z: 4, core: 2. Of those that a mesh axis runs over, the one named last changes fastest.
Arguments:
- embedding: bfloat16 [32, 196608], P(None, ('tm', 'cell')), may hold values from -4 to 4, as said below
- counts: int32 [32], replicated, may hold values from 384 to 6144, as said below
Outputs:
- gradient: float32 [32, 196608], P(None, ('tm', 'cell'))
Inputs may be any that keep to these rules, and one draw needn't show every extreme that they name: Time point t has counts[t] live cells in the first counts[t] of its 6144 slots; the other slots are padding. `embedding`: values of order one.
All inputs are finite; a program needn't handle non-finite values.
Results may differ from a plain program's by a relative error of at most 0.0013.
Values may be sent and summed in bfloat16 or wider, within the bound.
No kernel may reach another device: no remote copies, remote signals or barrier semaphores. Data moves between devices by JAX's collectives and lax.ppermute only.
A program may use at most 128 MiB of HBM per device.

v0:
```python
import jax
import jax.numpy as jnp
from jax import lax
from jax.sharding import PartitionSpec as P

SWEEPS = 2
ADJOINT = 2


ENTROPY = 0.25
PENALTY = 5.0
DAMPING = PENALTY / (PENALTY + ENTROPY)
MASKED = -1e30


def shifted(block, axis, distance):
    devices = range(lax.axis_size(axis))
    route = [(i - distance, i) for i in devices if i - distance in devices]
    return lax.ppermute(block, axis, route)


def joined(shard, axis, combine):
    everything = jax.tree.map(lambda part: lax.all_gather(part, axis), shard)
    initial = jax.tree.map(lambda part: part[0], everything)

    def turn(k, so_far):
        return combine(so_far, jax.tree.map(lambda part: part[k], everything))

    return lax.fori_loop(1, lax.axis_size(axis), turn, initial)


def cost_tile(sources, targets, source_sq, target_sq):
    products = lax.dot_general(
        sources, targets, (((0,), (0,)), ((), ())), preferred_element_type=jnp.float32
    )
    return source_sq[:, None] + target_sq[None, :] - 2.0 * products


def lse_combine(first, second):
    top_value = jnp.maximum(first[0], second[0])
    summed = first[1] * jnp.exp(first[0] - top_value) + second[1] * jnp.exp(second[0] - top_value)
    return (top_value, summed)


def final_combine(first, second):
    top_value, summed = lse_combine((first[0], first[1]), (second[0], second[1]))
    return (top_value, summed, first[2] + second[2])


def per_device(embedding, counts):
    feat_dim, local_rows = embedding.shape
    time_size = lax.axis_size("tm")
    group_size = lax.axis_size("cell")
    time_here = lax.axis_index("tm")
    member = lax.axis_index("cell")
    count_here = lax.dynamic_index_in_dim(counts, time_here, 0, keepdims=False)
    later_time = jnp.minimum(time_here + 1, time_size - 1)
    count_next = jnp.where(
        time_here + 1 < time_size,
        lax.dynamic_index_in_dim(counts, later_time, 0, keepdims=False),
        0,
    )
    local_ids = jnp.arange(local_rows, dtype=jnp.int32)
    grouped = lax.all_gather(embedding, "cell", axis=1, tiled=True)
    targets = shifted(grouped, "tm", -1)
    source_ids = member * local_rows + local_ids
    target_ids = jnp.arange(local_rows * group_size, dtype=jnp.int32)
    source_rows = embedding.shape[1]
    target_slots = targets.shape[1]
    source_live = source_ids < count_here
    target_live = target_ids < count_next
    step_rows = source_rows // max(1, source_rows // 768)
    num_blocks = source_rows // step_rows
    block_ids = jnp.arange(num_blocks, dtype=jnp.int32)
    source_f32 = embedding.astype(jnp.float32)
    target_f32 = targets.astype(jnp.float32)
    source_sq = jnp.sum(source_f32 * source_f32, axis=0)
    target_sq = jnp.sum(target_f32 * target_f32, axis=0)
    zero_cols = jnp.zeros((target_slots,), jnp.float32)
    masked_cols = jnp.full((target_slots,), MASKED, jnp.float32)

    def rows_of(vector, block_index):
        return lax.dynamic_slice_in_dim(vector, block_index * step_rows, step_rows, 0)

    def tile(block_index):
        piece = lax.dynamic_slice_in_dim(embedding, block_index * step_rows, step_rows, 1)
        mask = rows_of(source_live, block_index)[:, None] & target_live[None, :]
        return (piece, mask, cost_tile(piece, targets, rows_of(source_sq, block_index), target_sq))

    source_pot = jnp.zeros((source_rows,), jnp.float32)
    target_pot = zero_cols
    last_rows = jnp.zeros((source_rows,), jnp.float32)
    for sweep in range(SWEEPS):

        def column_visit(carry, block_index):
            piece, mask, cost = tile(block_index)
            scores = jnp.where(
                mask, (rows_of(source_pot, block_index)[:, None] - cost) / ENTROPY, MASKED
            )
            block_top = jnp.max(scores, axis=0)
            block_sum = jnp.sum(jnp.exp(scores - block_top[None, :]), axis=0)
            return (lse_combine(carry, (block_top, block_sum)), None)

        result, _ = lax.scan(column_visit, (masked_cols, zero_cols), block_ids)
        top_value, summed = joined((result[0], result[1]), "cell", lse_combine)
        target_pot = jnp.where(target_live, -DAMPING * ENTROPY * (top_value + jnp.log(summed)), 0.0)

        def row_visit(block_index):
            piece, mask, cost = tile(block_index)
            scores = jnp.where(mask, (target_pot[None, :] - cost) / ENTROPY, MASKED)
            block_top = jnp.max(scores, axis=1)
            return (block_top, jnp.sum(jnp.exp(scores - block_top[:, None]), axis=1))

        tops, sums = lax.map(row_visit, block_ids)
        row_top = tops.reshape(source_rows)
        row_sum = sums.reshape(source_rows)
        row_top, row_sum = (row_top, row_sum)
        last_rows = row_top + jnp.log(row_sum)
        source_pot = jnp.where(source_live, -DAMPING * ENTROPY * last_rows, 0.0)

    def stats_visit(carry, block_index):
        piece, mask, cost = tile(block_index)
        src_pot = rows_of(source_pot, block_index)
        plan = jnp.where(
            mask, jnp.exp((src_pot[:, None] + target_pot[None, :] - cost) / ENTROPY), 0.0
        )
        scores = jnp.where(mask, (src_pot[:, None] - cost) / ENTROPY, MASKED)
        block_top = jnp.max(scores, axis=0)
        block_sum = jnp.sum(jnp.exp(scores - block_top[None, :]), axis=0)
        weighted = plan * cost / ENTROPY
        top_value, summed = lse_combine((carry[0], carry[1]), (block_top, block_sum))
        return (
            (top_value, summed, carry[2] + jnp.sum(weighted, axis=0)),
            jnp.sum(weighted, axis=1),
        )

    partial_stats, pushes = lax.scan(stats_visit, (masked_cols, zero_cols, zero_cols), block_ids)
    top_value, summed, target_push = joined(
        (partial_stats[0], partial_stats[1], partial_stats[2]), "cell", final_combine
    )
    final_cols = top_value + jnp.log(summed)
    source_push = pushes.reshape(source_rows)

    def kernels(block_index):
        piece, mask, cost = tile(block_index)
        src_pot = rows_of(source_pot, block_index)
        src_log = rows_of(last_rows, block_index)
        plan = jnp.where(
            mask, jnp.exp((src_pot[:, None] + target_pot[None, :] - cost) / ENTROPY), 0.0
        )
        row_kernel = jnp.where(
            mask, jnp.exp((target_pot[None, :] - cost) / ENTROPY - src_log[:, None]), 0.0
        )
        col_kernel = jnp.where(
            mask, jnp.exp((src_pot[:, None] - cost) / ENTROPY - final_cols[None, :]), 0.0
        )
        return (piece, cost, plan, row_kernel, col_kernel)

    source_adj, target_adj = (source_push, target_push)
    for step_k in range(ADJOINT):
        prior_rows, prior_cols = (source_adj, target_adj)

        def adj_visit(carry, block_index):
            piece, cost, plan, row_kernel, col_kernel = kernels(block_index)
            row_part = jnp.sum(col_kernel * prior_cols[None, :], axis=1)
            return (
                carry + jnp.sum(row_kernel * rows_of(prior_rows, block_index)[:, None], axis=0),
                row_part,
            )

        col_part, row_parts = lax.scan(adj_visit, zero_cols, block_ids)
        source_adj = source_push - DAMPING * row_parts.reshape(source_rows)
        target_adj = target_push - DAMPING * lax.psum(col_part, "cell")

    def grad_visit(carry, block_index):
        piece, cost, plan, row_kernel, col_kernel = kernels(block_index)
        adj_rows = rows_of(source_adj, block_index)
        cost_grad = plan * (1.0 - cost / ENTROPY) + DAMPING * (
            adj_rows[:, None] * row_kernel + target_adj[None, :] * col_kernel
        )
        rounded = cost_grad.astype(jnp.bfloat16)
        row_total = jnp.sum(cost_grad, axis=1)
        pulled_rows = lax.dot_general(
            targets, rounded, (((1,), (1,)), ((), ())), preferred_element_type=jnp.float32
        )
        src_cols = lax.dynamic_slice_in_dim(source_f32, block_index * step_rows, step_rows, 1)
        source_grad = 2.0 * (src_cols * row_total[None, :] - pulled_rows)
        pulled_cols = lax.dot_general(
            piece, rounded, (((1,), (0,)), ((), ())), preferred_element_type=jnp.float32
        )
        return ((carry[0] + jnp.sum(cost_grad, axis=0), carry[1] + pulled_cols), source_grad)

    start_pair = (zero_cols, jnp.zeros((feat_dim, target_slots), jnp.float32))
    (col_total, pulled_total), source_grads = lax.scan(grad_visit, start_pair, block_ids)
    source_grad = jnp.transpose(source_grads, (1, 0, 2)).reshape(feat_dim, source_rows)
    target_part = 2.0 * (target_f32 * col_total[None, :] - pulled_total)
    arrived = shifted(target_part, "tm", 1)
    incoming = lax.psum_scatter(arrived, "cell", scatter_dimension=1, tiled=True)
    return source_grad + incoming


def solution(mesh):
    in_specs = (P(None, ("tm", "cell")), P())
    out_specs = P(None, ("tm", "cell"))
    return jax.shard_map(
        per_device, mesh=mesh, in_specs=in_specs, out_specs=out_specs, check_vma=False
    )
```

profile of v0, /device:TPU:68, one launch (start us, length us, event | category | flops | bytes accessed | tf_op | source)
XLA Modules:
  0.0 553.8 jit_solution(11797713500677597081)
XLA Ops:
  6.5 8.4 %all_gather.45 = bf16[32,6144]{1,0:T(8,128)(2,1)S(1)} all-gather(bf16[32,1536]{1,0:T(8,128)(2,1)} %param.24), channel_id=1, replica_groups=mesh['tm'=32,'cell'=4] {'cell'}, dimensions={1}, use_global_device_ids=true | all-gather | bytes 491520 | tf_op jit(solution)/shard_map/all_gather | solution.py:64
  28.3 41.9 %while.168 = (s32[]{:T(128)}, f32[6144]{0:T(1024)S(1)}, f32[6144]{0:T(1024)S(1)}, s32[2]{0:T(128)S(1)}, pred[1536]{0:T(1024)(128)(4,1)S(1)}, /*index=5*/f32[1536...) while((s32[]{:T(128)}, f32[6144]{0:T(1024)S(1)}, ...), condition=%wide.region_5.6_spmd.clone, body=%wide.region_2.5_spmd.clone.sunk | while | flops 349218816 | bytes 38460888 | solution.py:104
  29.8 10.4 %fusion.127 = (f32[6144]{0:T(1024)S(1)}, f32[768,6144]{1,0:T(8,128)}) fusion(bf16[32,6144]{1,0:T(8,128)(2,1)S(1)} %get-tuple-element.2542, bf16[32,1536]{1,0:T(8,128)(2,1)} %get-tuple-element.2541, s32[]{:T(128)S(6)} %select_n.256, f32[6144]{0:T(1024)S(1)} %get-tuple-element.2540, f32[768]{0:T(1024)S(1)} %dynamic_slice.363, ...), kind=kOutput, calls=%fused_computation.130.clone.1 | convolution fusion | flops 339732480 | bytes 19375876 | tf_op jit(solution)/shard_map/while/body/eval_jaxpr/dot_general | solution.py:33
  40.3 8.9 %exponential_reduce_fusion.11 = f32[6144]{0:T(1024)S(1)} fusion(f32[768,6144]{1,0:T(8,128)} %get-tuple-element.2407, f32[6144]{0:T(1024)S(1)} %get-tuple-element.2408), kind=kLoop, calls=%fused_computation.28.clone.1 | loop fusion | flops 9431040 | bytes 18923520 | tf_op jit(solution)/shard_map/while/body/eval_jaxpr/reduce_sum | solution.py:101
  50.8 10.4 %fusion.127 = (f32[6144]{0:T(1024)S(1)}, f32[768,6144]{1,0:T(8,128)}) fusion(bf16[32,6144]{1,0:T(8,128)(2,1)S(1)} %get-tuple-element.2542, bf16[32,1536]{1,0:T(8,128)(2,1)} %get-tuple-element.2541, s32[]{:T(128)S(6)} %select_n.256, f32[6144]{0:T(1024)S(1)} %get-tuple-element.2540, f32[768]{0:T(1024)S(1)} %dynamic_slice.363, ...), kind=kOutput, calls=%fused_computation.130.clone.1 | convolution fusion | flops 339732480 | bytes 19375876 | tf_op jit(solution)/shard_map/while/body/eval_jaxpr/dot_general | solution.py:33
  61.2 8.9 %exponential_reduce_fusion.11 = f32[6144]{0:T(1024)S(1)} fusion(f32[768,6144]{1,0:T(8,128)} %get-tuple-element.2407, f32[6144]{0:T(1024)S(1)} %get-tuple-element.2408), kind=kLoop, calls=%fused_computation.28.clone.1 | loop fusion | flops 9431040 | bytes 18923520 | tf_op jit(solution)/shard_map/while/body/eval_jaxpr/reduce_sum | solution.py:101
  70.2 6.8 %all-gather = f32[24576]{0:T(1024)S(1)} all-gather(f32[6144]{0:T(1024)S(1)} %get-tuple-element.1011), channel_id=2, replica_groups=mesh['tm'=32,'cell'=4] {'cell'}, dimensions={0}, use_global_device_ids=true | all-gather | bytes 122880 | tf_op jit(solution)/shard_map/all_gather | solution.py:23
  77.1 7.1 %all-gather.1 = f32[24576]{0:T(1024)S(1)} all-gather(f32[6144]{0:T(1024)S(1)} %get-tuple-element.1012), channel_id=3, replica_groups=mesh['tm'=32,'cell'=4] {'cell'}, dimensions={0}, use_global_device_ids=true | all-gather | bytes 122880 | tf_op jit(solution)/shard_map/all_gather | solution.py:23
  84.6 42.5 %while.166 = (s32[]{:T(128)}, f32[2,768]{1,0:T(2,128)S(1)}, f32[2,768]{1,0:T(2,128)S(1)}, s32[2]{0:T(128)S(1)}, pred[1536]{0:T(1024)(128)(4,1)S(1)}, /*index=5*/...) while((s32[]{:T(128)}, f32[2,768]{1,0:T(2,128)S(1)}, ...), condition=%wide.region_11.12_spmd.clone, body=%wide.region_8.11_spmd.clone.sunk | while | flops 349180416 | bytes 38298076 | solution.py:114
  86.1 10.6 %fusion.123 = (f32[768]{0:T(1024)S(1)}, f32[768,6144]{1,0:T(8,128)}) fusion(bf16[32,6144]{1,0:T(8,128)(2,1)S(1)} %get-tuple-element.2611, bf16[32,1536]{1,0:T(8,128)(2,1)} %get-tuple-element.2610, s32[]{:T(128)S(6)} %select_n.254, f32[6144]{0:T(1024)S(1)} %get-tuple-element.2609, f32[768]{0:T(1024)S(1)} %dynamic_slice.355, ...), kind=kOutput, calls=%fused_computation.128.clone.1 | convolution fusion | flops 339737856 | bytes 19378948 | tf_op jit(solution)/shard_map/while/body/eval_jaxpr/dot_general | solution.py:33
  96.7 9.0 %exponential_reduce_fusion.9 = f32[768]{0:T(1024)S(1)} fusion(f32[768,6144]{1,0:T(8,128)} %get-tuple-element.2383, f32[768]{0:T(1024)S(1)} %get-tuple-element.2382), kind=kLoop, calls=%fused_computation.18.clone.1 | loop fusion | flops 9436416 | bytes 18880512 | tf_op jit(solution)/shard_map/while/body/eval_jaxpr/reduce_sum | solution.py:112
  107.4 10.6 %fusion.123 = (f32[768]{0:T(1024)S(1)}, f32[768,6144]{1,0:T(8,128)}) fusion(bf16[32,6144]{1,0:T(8,128)(2,1)S(1)} %get-tuple-element.2611, bf16[32,1536]{1,0:T(8,128)(2,1)} %get-tuple-element.2610, s32[]{:T(128)S(6)} %select_n.254, f32[6144]{0:T(1024)S(1)} %get-tuple-element.2609, f32[768]{0:T(1024)S(1)} %dynamic_slice.355, ...), kind=kOutput, calls=%fused_computation.128.clone.1 | convolution fusion | flops 339737856 | bytes 19378948 | tf_op jit(solution)/shard_map/while/body/eval_jaxpr/dot_general | solution.py:33
  118.0 9.0 %exponential_reduce_fusion.9 = f32[768]{0:T(1024)S(1)} fusion(f32[768,6144]{1,0:T(8,128)} %get-tuple-element.2383, f32[768]{0:T(1024)S(1)} %get-tuple-element.2382), kind=kLoop, calls=%fused_computation.18.clone.1 | loop fusion | flops 9436416 | bytes 18880512 | tf_op jit(solution)/shard_map/while/body/eval_jaxpr/reduce_sum | solution.py:112
  127.8 43.1 %while.169 = (s32[]{:T(128)}, f32[6144]{0:T(1024)S(1)}, f32[6144]{0:T(1024)S(1)}, s32[2]{0:T(128)S(1)}, pred[1536]{0:T(1024)(128)(4,1)S(1)}, /*index=5*/f32[1536...) while((s32[]{:T(128)}, f32[6144]{0:T(1024)S(1)}, ...), condition=%wide.region_15.16_spmd.clone, body=%wide.region_12.15_spmd.clone.sunk | while | flops 349218816 | bytes 38470112 | solution.py:104
  129.6 11.0 %fusion.130 = (f32[6144]{0:T(1024)S(1)}, f32[768,6144]{1,0:T(8,128)}) fusion(bf16[32,6144]{1,0:T(8,128)(2,1)S(1)} %get-tuple-element.2656, bf16[32,1536]{1,0:T(8,128)(2,1)} %get-tuple-element.2655, s32[]{:T(128)S(6)} %select_n.257, f32[6144]{0:T(1024)S(1)} %get-tuple-element.2654, f32[768]{0:T(1024)S(1)} %dynamic_slice.367, ...), kind=kOutput, calls=%fused_computation.131.clone.1 | convolution fusion | flops 339732480 | bytes 19378948 | tf_op jit(solution)/shard_map/while/body/eval_jaxpr/dot_general | solution.py:33
  140.5 8.9 %exponential_reduce_fusion.12 = f32[6144]{0:T(1024)S(1)} fusion(f32[768,6144]{1,0:T(8,128)} %get-tuple-element.2422, f32[6144]{0:T(1024)S(1)} %get-tuple-element.2423), kind=kLoop, calls=%fused_computation.36.clone.1 | loop fusion | flops 9431040 | bytes 18923520 | tf_op jit(solution)/shard_map/while/body/eval_jaxpr/reduce_sum | solution.py:101
  151.0 11.0 %fusion.130 = (f32[6144]{0:T(1024)S(1)}, f32[768,6144]{1,0:T(8,128)}) fusion(bf16[32,6144]{1,0:T(8,128)(2,1)S(1)} %get-tuple-element.2656, bf16[32,1536]{1,0:T(8,128)(2,1)} %get-tuple-element.2655, s32[]{:T(128)S(6)} %select_n.257, f32[6144]{0:T(1024)S(1)} %get-tuple-element.2654, f32[768]{0:T(1024)S(1)} %dynamic_slice.367, ...), kind=kOutput, calls=%fused_computation.131.clone.1 | convolution fusion | flops 339732480 | bytes 19378948 | tf_op jit(solution)/shard_map/while/body/eval_jaxpr/dot_general | solution.py:33
  161.9 8.9 %exponential_reduce_fusion.12 = f32[6144]{0:T(1024)S(1)} fusion(f32[768,6144]{1,0:T(8,128)} %get-tuple-element.2422, f32[6144]{0:T(1024)S(1)} %get-tuple-element.2423), kind=kLoop, calls=%fused_computation.36.clone.1 | loop fusion | flops 9431040 | bytes 18923520 | tf_op jit(solution)/shard_map/while/body/eval_jaxpr/reduce_sum | solution.py:101
  170.9 6.8 %all-gather.2 = f32[24576]{0:T(1024)S(1)} all-gather(f32[6144]{0:T(1024)S(1)} %get-tuple-element.1017), channel_id=4, replica_groups=mesh['tm'=32,'cell'=4] {'cell'}, dimensions={0}, use_global_device_ids=true | all-gather | bytes 122880 | tf_op jit(solution)/shard_map/all_gather | solution.py:23
  177.8 6.8 %all-gather.3 = f32[24576]{0:T(1024)S(1)} all-gather(f32[6144]{0:T(1024)S(1)} %get-tuple-element.1018), channel_id=5, replica_groups=mesh['tm'=32,'cell'=4] {'cell'}, dimensions={0}, use_global_device_ids=true | all-gather | bytes 122880 | tf_op jit(solution)/shard_map/all_gather | solution.py:23
  185.6 42.2 %while.167 = (s32[]{:T(128)}, f32[2,768]{1,0:T(2,128)S(1)}, f32[2,768]{1,0:T(2,128)S(1)}, s32[2]{0:T(128)S(1)}, pred[1536]{0:T(1024)(128)(4,1)S(1)}, /*index=5*/...) while((s32[]{:T(128)}, f32[2,768]{1,0:T(2,128)S(1)}, ...), condition=%wide.region_21.22_spmd.clone, body=%wide.region_18.21_spmd.clone.sunk | while | flops 349180416 | bytes 38298076 | solution.py:114
  187.0 10.6 %fusion.125 = (f32[768]{0:T(1024)S(1)}, f32[768,6144]{1,0:T(8,128)}) fusion(bf16[32,6144]{1,0:T(8,128)(2,1)S(1)} %get-tuple-element.2725, bf16[32,1536]{1,0:T(8,128)(2,1)} %get-tuple-element.2724, s32[]{:T(128)S(6)} %select_n.255, f32[6144]{0:T(1024)S(1)} %get-tuple-element.2723, f32[768]{0:T(1024)S(1)} %dynamic_slice.359, ...), kind=kOutput, calls=%fused_computation.129.clone.1 | convolution fusion | flops 339737856 | bytes 19378948 | tf_op jit(solution)/shard_map/while/body/eval_jaxpr/dot_general | solution.py:33
  197.6 9.0 %exponential_reduce_fusion.10 = f32[768]{0:T(1024)S(1)} fusion(f32[768,6144]{1,0:T(8,128)} %get-tuple-element.2396, f32[768]{0:T(1024)S(1)} %get-tuple-element.2395), kind=kLoop, calls=%fused_computation.23.clone.1 | loop fusion | flops 9436416 | bytes 18880512 | tf_op jit(solution)/shard_map/while/body/eval_jaxpr/reduce_sum | solution.py:112
  208.1 10.6 %fusion.125 = (f32[768]{0:T(1024)S(1)}, f32[768,6144]{1,0:T(8,128)}) fusion(bf16[32,6144]{1,0:T(8,128)(2,1)S(1)} %get-tuple-element.2725, bf16[32,1536]{1,0:T(8,128)(2,1)} %get-tuple-element.2724, s32[]{:T(128)S(6)} %select_n.255, f32[6144]{0:T(1024)S(1)} %get-tuple-element.2723, f32[768]{0:T(1024)S(1)} %dynamic_slice.359, ...), kind=kOutput, calls=%fused_computation.129.clone.1 | convolution fusion | flops 339737856 | bytes 19378948 | tf_op jit(solution)/shard_map/while/body/eval_jaxpr/dot_general | solution.py:33
  218.7 9.0 %exponential_reduce_fusion.10 = f32[768]{0:T(1024)S(1)} fusion(f32[768,6144]{1,0:T(8,128)} %get-tuple-element.2396, f32[768]{0:T(1024)S(1)} %get-tuple-element.2395), kind=kLoop, calls=%fused_computation.23.clone.1 | loop fusion | flops 9436416 | bytes 18880512 | tf_op jit(solution)/shard_map/while/body/eval_jaxpr/reduce_sum | solution.py:112
  228.6 65.9 %while.170 = (s32[]{:T(128)}, f32[6144]{0:T(1024)S(1)}, f32[6144]{0:T(1024)S(1)}, f32[6144]{0:T(1024)S(1)}, f32[2,768]{1,0:T(2,128)S(1)}, /*index=5*/s32[2]{0:T(...) while((s32[]{:T(128)}, f32[6144]{0:T(1024)S(1)}, ...), condition=%wide.region_27.28_spmd.clone, body=%wide.region_22.27_spmd.clone.sunk | while | flops 420003072 | bytes 76394744 | solution.py:137
  230.2 7.1 %fusion.133 = (f32[6144]{0:T(1024)S(1)}, f32[768,6144]{1,0:T(8,128)S(1)}) fusion(f32[6144]{0:T(1024)S(1)} %get-tuple-element.2776, f32[768]{0:T(1024)S(1)} %dynamic_slice.372, f32[768]{0:T(1024)S(1)} %dynamic_slice.373, pred[6144]{0:T(1024)(128)(4,1)S(1)} %iota_compare_fusion.21, pred[768]{0:T(1024)(128)(4,1)S(1)} %dynamic_slice.374, ...), kind=kOutput, calls=%fused_computation.50.clone.1 | convolution fusion | flops 339732480 | bytes 19378948 | tf_op jit(solution)/shard_map/while/body/eval_jaxpr/dot_general | solution.py:33
  237.3 14.9 %fusion.134 = (f32[768,6144]{1,0:T(8,128)}, f32[6144]{0:T(1024)S(1)}) fusion(f32[768,6144]{1,0:T(8,128)S(1)} %get-tuple-element.2440, f32[6144]{0:T(1024)S(1)} %get-tuple-element.2779, f32[6144]{0:T(1024)S(1)} %get-tuple-element.2776, f32[768]{0:T(1024)S(1)} %dynamic_slice.372, f32[768]{0:T(1024)S(1)} %dynamic_slice.373, ...), kind=kLoop, calls=%fused_computation.47.clone.1 | loop fusion | flops 70772736 | bytes 37860096 | tf_op jit(solution)/shard_map/while/body/eval_jaxpr/div | solution.py:130
  252.2 9.3 %fusion.135 = (f32[768]{0:T(1024)S(1)}, f32[6144]{0:T(1024)S(1)}) fusion(f32[768,6144]{1,0:T(8,128)} %get-tuple-element.2443), kind=kLoop, calls=%fused_computation.126.clone.1 | loop fusion | flops 9430272 | bytes 18902016 | tf_op jit(solution)/shard_map/while/body/eval_jaxpr/reduce_sum | solution.py:134
  263.0 7.1 %fusion.133 = (f32[6144]{0:T(1024)S(1)}, f32[768,6144]{1,0:T(8,128)S(1)}) fusion(f32[6144]{0:T(1024)S(1)} %get-tuple-element.2776, f32[768]{0:T(1024)S(1)} %dynamic_slice.372, f32[768]{0:T(1024)S(1)} %dynamic_slice.373, pred[6144]{0:T(1024)(128)(4,1)S(1)} %iota_compare_fusion.21, pred[768]{0:T(1024)(128)(4,1)S(1)} %dynamic_slice.374, ...), kind=kOutput, calls=%fused_computation.50.clone.1 | convolution fusion | flops 339732480 | bytes 19378948 | tf_op jit(solution)/shard_map/while/body/eval_jaxpr/dot_general | solution.py:33
  270.2 14.9 %fusion.134 = (f32[768,6144]{1,0:T(8,128)}, f32[6144]{0:T(1024)S(1)}) fusion(f32[768,6144]{1,0:T(8,128)S(1)} %get-tuple-element.2440, f32[6144]{0:T(1024)S(1)} %get-tuple-element.2779, f32[6144]{0:T(1024)S(1)} %get-tuple-element.2776, f32[768]{0:T(1024)S(1)} %dynamic_slice.372, f32[768]{0:T(1024)S(1)} %dynamic_slice.373, ...), kind=kLoop, calls=%fused_computation.47.clone.1 | loop fusion | flops 70772736 | bytes 37860096 | tf_op jit(solution)/shard_map/while/body/eval_jaxpr/div | solution.py:130
  285.1 9.3 %fusion.135 = (f32[768]{0:T(1024)S(1)}, f32[6144]{0:T(1024)S(1)}) fusion(f32[768,6144]{1,0:T(8,128)} %get-tuple-element.2443), kind=kLoop, calls=%fused_computation.126.clone.1 | loop fusion | flops 9430272 | bytes 18902016 | tf_op jit(solution)/shard_map/while/body/eval_jaxpr/reduce_sum | solution.py:134
  294.5 6.8 %all-gather.4 = f32[24576]{0:T(1024)S(1)} all-gather(f32[6144]{0:T(1024)S(1)} %get-tuple-element.1024), channel_id=6, replica_groups=mesh['tm'=32,'cell'=4] {'cell'}, dimensions={0}, use_global_device_ids=true | all-gather | bytes 122880 | tf_op jit(solution)/shard_map/all_gather | solution.py:23
  301.4 7.1 %all-gather.5 = f32[24576]{0:T(1024)S(1)} all-gather(f32[6144]{0:T(1024)S(1)} %get-tuple-element.1025), channel_id=7, replica_groups=mesh['tm'=32,'cell'=4] {'cell'}, dimensions={0}, use_global_device_ids=true | all-gather | bytes 122880 | tf_op jit(solution)/shard_map/all_gather | solution.py:23
  308.5 6.8 %all-gather.6 = f32[24576]{0:T(1024)S(1)} all-gather(f32[6144]{0:T(1024)S(1)} %get-tuple-element.1026), channel_id=8, replica_groups=mesh['tm'=32,'cell'=4] {'cell'}, dimensions={0}, use_global_device_ids=true | all-gather | bytes 122880 | tf_op jit(solution)/shard_map/all_gather | solution.py:23
  315.9 34.6 %while.171 = (s32[]{:T(128)}, f32[6144]{0:T(1024)S(1)}, f32[2,768]{1,0:T(2,128)S(1)}, s32[2]{0:T(128)S(1)}, pred[1536]{0:T(1024)(128)(4,1)S(1)}, /*index=5*/f32[...) while((s32[]{:T(128)}, f32[6144]{0:T(1024)S(1)}, ...), condition=%wide.region_33.34_spmd.clone, body=%wide.region_30.33_spmd.clone.sunk | while | flops 377498880 | bytes 706073 | solution.py:171
  317.6 15.6 %fusion.138 = (f32[768]{0:T(1024)S(1)}, f32[6144]{0:T(1024)S(1)}) fusion(f32[6144]{0:T(1024)S(1)} %get-tuple-element.2869, f32[6144]{0:T(1024)S(1)} %get-tuple-element.2868, f32[768]{0:T(1024)S(1)} %dynamic_slice.377, f32[6144]{0:T(1024)S(1)} %get-tuple-element.2862, f32[768]{0:T(1024)S(1)} %dynamic_slice.378, ...), kind=kOutput, calls=%fused_computation.64.clone.1 | convolution fusion | flops 377480448 | bytes 587524 | tf_op jit(solution)/shard_map/while/body/eval_jaxpr/dot_general | solution.py:33
  334.9 15.6 %fusion.138 = (f32[768]{0:T(1024)S(1)}, f32[6144]{0:T(1024)S(1)}) fusion(f32[6144]{0:T(1024)S(1)} %get-tuple-element.2869, f32[6144]{0:T(1024)S(1)} %get-tuple-element.2868, f32[768]{0:T(1024)S(1)} %dynamic_slice.377, f32[6144]{0:T(1024)S(1)} %get-tuple-element.2862, f32[768]{0:T(1024)S(1)} %dynamic_slice.378, ...), kind=kOutput, calls=%fused_computation.64.clone.1 | convolution fusion | flops 377480448 | bytes 587524 | tf_op jit(solution)/shard_map/while/body/eval_jaxpr/dot_general | solution.py:33
  350.6 15.8 %psum.14 = f32[6144]{0:T(1024)S(1)} all-reduce(f32[6144]{0:T(1024)S(1)} %get-tuple-element.1031), channel_id=1, replica_groups=mesh['tm'=32,'cell'=4] {'cell'}, use_global_device_ids=true, to_apply=%region_34.35 | all-reduce | flops 6144 | bytes 49152 | tf_op jit(solution)/shard_map/psum | solution.py:173
  366.5 34.7 %while.172 = (s32[]{:T(128)}, f32[6144]{0:T(1024)S(1)}, f32[2,768]{1,0:T(2,128)S(1)}, s32[2]{0:T(128)S(1)}, pred[1536]{0:T(1024)(128)(4,1)S(1)}, /*index=5*/f32[...) while((s32[]{:T(128)}, f32[6144]{0:T(1024)S(1)}, ...), condition=%wide.region_38.39_spmd.clone, body=%wide.region_35.38_spmd.clone.sunk | while | flops 377498880 | bytes 706073 | solution.py:171
  368.1 15.6 %fusion.140 = (f32[768]{0:T(1024)S(1)}, f32[6144]{0:T(1024)S(1)}) fusion(f32[6144]{0:T(1024)S(1)} %get-tuple-element.2929, f32[6144]{0:T(1024)S(1)} %get-tuple-element.2928, f32[768]{0:T(1024)S(1)} %dynamic_slice.384, f32[6144]{0:T(1024)S(1)} %get-tuple-element.2922, f32[768]{0:T(1024)S(1)} %dynamic_slice.385, ...), kind=kOutput, calls=%fused_computation.76.clone.1 | convolution fusion | flops 377480448 | bytes 587524 | tf_op jit(solution)/shard_map/while/body/eval_jaxpr/dot_general | solution.py:33
  385.5 15.6 %fusion.140 = (f32[768]{0:T(1024)S(1)}, f32[6144]{0:T(1024)S(1)}) fusion(f32[6144]{0:T(1024)S(1)} %get-tuple-element.2929, f32[6144]{0:T(1024)S(1)} %get-tuple-element.2928, f32[768]{0:T(1024)S(1)} %dynamic_slice.384, f32[6144]{0:T(1024)S(1)} %get-tuple-element.2922, f32[768]{0:T(1024)S(1)} %dynamic_slice.385, ...), kind=kOutput, calls=%fused_computation.76.clone.1 | convolution fusion | flops 377480448 | bytes 587524 | tf_op jit(solution)/shard_map/while/body/eval_jaxpr/dot_general | solution.py:33
  401.2 13.5 %psum.15 = f32[6144]{0:T(1024)S(1)} all-reduce(f32[6144]{0:T(1024)S(1)} %get-tuple-element.1033), channel_id=1, replica_groups=mesh['tm'=32,'cell'=4] {'cell'}, use_global_device_ids=true, to_apply=%region_39.40 | all-reduce | flops 6144 | bytes 49152 | tf_op jit(solution)/shard_map/psum | solution.py:173
  414.9 74.8 %while.173 = (s32[]{:T(128)}, f32[6144]{0:T(1024)S(1)}, f32[32,6144]{1,0:T(8,128)S(1)}, f32[2,32,768]{2,1,0:T(8,128)S(1)}, s32[2]{0:T(128)S(1)}, /*index=5*/pred...) while((s32[]{:T(128)}, f32[6144]{0:T(1024)S(1)}, ...), condition=%wide.region_43.44_spmd.clone, body=%wide.region_40.43_spmd.clone.sunk | while | flops 1033850112 | bytes 69363304 | solution.py:194
  416.5 23.8 %fusion.146 = (f32[768]{0:T(1024)S(1)}, f32[6144]{0:T(1024)S(1)}, bf16[768,6144]{1,0:T(8,128)(2,1)S(1)}) fusion(f32[6144]{0:T(1024)S(1)} %get-tuple-element.2994, f32[6144]{0:T(1024)S(1)} %get-tuple-element.2993, f32[768]{0:T(1024)S(1)} %dynamic_slice.393, f32[768]{0:T(1024)S(1)} %dynamic_slice.394, bf16[32,6144]{1,0:T(8,128)(2,1)S(1)} %get-tuple-element.2990, ...), kind=kOutput, calls=%fused_computation.127.clone.1 | convolution fusion | flops 429384960 | bytes 10024708 | tf_op jit(solution)/shard_map/while/body/eval_jaxpr/dot_general | solution.py:33
  453.9 23.8 %fusion.146 = (f32[768]{0:T(1024)S(1)}, f32[6144]{0:T(1024)S(1)}, bf16[768,6144]{1,0:T(8,128)(2,1)S(1)}) fusion(f32[6144]{0:T(1024)S(1)} %get-tuple-element.2994, f32[6144]{0:T(1024)S(1)} %get-tuple-element.2993, f32[768]{0:T(1024)S(1)} %dynamic_slice.393, f32[768]{0:T(1024)S(1)} %dynamic_slice.394, bf16[32,6144]{1,0:T(8,128)(2,1)S(1)} %get-tuple-element.2990, ...), kind=kOutput, calls=%fused_computation.127.clone.1 | convolution fusion | flops 429384960 | bytes 10024708 | tf_op jit(solution)/shard_map/while/body/eval_jaxpr/dot_general | solution.py:33
  493.3 18.8 %collective-permute-done.1 = f32[32,6144]{1,0:T(8,128)S(1)} collective-permute-done((f32[32,6144]{1,0:T(8,128)S(1)}, f32[32,6144]{1,0:T(8,128)S(1)}, u32[]{:S(2)}, u32[]{:S(2)}) %collective-permute-start.1) | collective-permute-done | bytes 786464 | tf_op jit(solution)/shard_map/ppermute | solution.py:19
  513.0 31.9 %reduce-scatter.2.cloned.1.call-done = f32[32,1536]{1,0:T(8,128)} async-done(((f32[32,6144]{1,0:T(8,128)}), f32[32,1536]{1,0:T(8,128)}) %reduce-scatter.2.cloned.1.call-update) | async-done | bytes 196624 | tf_op jit(solution)/shard_map/reduce_scatter | solution.py:198
  (261 shorter events, 62.0 us)
Async XLA Ops:
  6.5 538.4 %reduce-scatter.2.cloned.1.call-start = ((), (), s32[]{:S(2)}) async-start(), calls=%async_computation.1 | async-start | bytes 983040 | tf_op jit(solution)/shard_map/reduce_scatter | solution.py:198
  14.9 13.2 %collective-permute-start = (bf16[32,6144]{1,0:T(8,128)(2,1)S(1)}, bf16[32,6144]{1,0:T(8,128)(2,1)S(1)}, u32[]{:S(2)}, u32[]{:S(2)}) collective-permute-start(bf16[32,6144]{1,0:T(8,128)(2,1)S(1)} %all_gather.45), channel_id=1, source_target_pairs={{4,0},{8,4},{12,8},{16,12},{20,16},{24,20},{28,24},{32,28},{36,32}... | collective-permute-start | bytes 1179656 | tf_op jit(solution)/shard_map/ppermute | solution.py:19
  84.6 43.2 %copy-start.8 = (f32[6144]{0:T(1024)S(1)}, f32[6144]{0:T(1024)}, u32[]{:S(2)}) copy-start(f32[6144]{0:T(1024)} %custom-call.2) | copy-start | bytes 73732
  84.6 43.2 %copy-start.9 = (f32[6144]{0:T(1024)S(1)}, f32[6144]{0:T(1024)}, u32[]{:S(2)}) copy-start(f32[6144]{0:T(1024)} %custom-call.3) | copy-start | bytes 73732
  185.6 43.0 %copy-start.5 = (f32[6144]{0:T(1024)S(1)}, f32[6144]{0:T(1024)}, u32[]{:S(2)}) copy-start(f32[6144]{0:T(1024)} %custom-call.4) | copy-start | bytes 73732
  185.6 43.0 %copy-start.6 = (f32[6144]{0:T(1024)S(1)}, f32[6144]{0:T(1024)}, u32[]{:S(2)}) copy-start(f32[6144]{0:T(1024)} %custom-call.5) | copy-start | bytes 73732
  185.6 43.0 %copy-start.7 = (f32[6144]{0:T(1024)S(1)}, f32[6144]{0:T(1024)}, u32[]{:S(2)}) copy-start(f32[6144]{0:T(1024)} %custom-call.6) | copy-start | bytes 73732
  228.5 87.4 %copy-start.11 = (f32[6144]{0:T(1024)S(1)}, f32[6144]{0:T(1024)}, u32[]{:S(2)}) copy-start(f32[6144]{0:T(1024)} %custom-call.7) | copy-start | bytes 73732
  315.9 50.5 %copy-start.10 = (f32[6144]{0:T(1024)S(1)}, f32[6144]{0:T(1024)}, u32[]{:S(2)}) copy-start(f32[6144]{0:T(1024)} %custom-call.8) | copy-start | bytes 73732
  366.4 48.4 %copy-start.1 = (f32[32,6144]{1,0:T(8,128)S(1)}, f32[32,6144]{1,0:T(8,128)}, u32[]{:S(2)}) copy-start(f32[32,6144]{1,0:T(8,128)} %custom-call.10) | copy-start | bytes 2359300
  366.4 48.4 %copy-start.3 = (f32[32,1536]{1,0:T(8,128)S(1)}, f32[32,1536]{1,0:T(8,128)}, u32[]{:S(2)}) copy-start(f32[32,1536]{1,0:T(8,128)} %convert_element_type.9) | copy-start | bytes 589828
  366.4 48.4 %copy-start.4 = (f32[6144]{0:T(1024)S(1)}, f32[6144]{0:T(1024)}, u32[]{:S(2)}) copy-start(f32[6144]{0:T(1024)} %custom-call.9) | copy-start | bytes 73732
  366.4 48.4 %copy-start.13 = (f32[2,32,768]{2,1,0:T(8,128)S(1)}, f32[2,32,768]{2,1,0:T(8,128)}, u32[]{:S(2)}) copy-start(f32[2,32,768]{2,1,0:T(8,128)} %custom-call.11) | copy-start | bytes 589828
  416.5 30.3 %copy-start.2 = (bf16[32,1536]{1,0:T(8,128)(2,1)S(1)}, bf16[32,1536]{1,0:T(8,128)(2,1)}, u32[]{:S(2)}) copy-start(bf16[32,1536]{1,0:T(8,128)(2,1)} %get-tuple-element.2989) | copy-start | bytes 294916 | tf_op jit(solution)/shard_map/while
  440.3 3.6 copy-start
  453.9 30.3 %copy-start.2 = (bf16[32,1536]{1,0:T(8,128)(2,1)S(1)}, bf16[32,1536]{1,0:T(8,128)(2,1)}, u32[]{:S(2)}) copy-start(bf16[32,1536]{1,0:T(8,128)(2,1)} %get-tuple-element.2989) | copy-start | bytes 294916 | tf_op jit(solution)/shard_map/while
  477.7 3.6 copy-start
  489.8 22.3 %collective-permute-start.1 = (f32[32,6144]{1,0:T(8,128)S(1)}, f32[32,6144]{1,0:T(8,128)S(1)}, u32[]{:S(2)}, u32[]{:S(2)}) collective-permute-start(f32[32,6144]{1,0:T(8,128)S(1)} %fusion.77), channel_id=1, source_target_pairs={{0,4},{4,8},{8,12},{12,16},{16,20},{20,24},{24,28},{28,32},{32,36}... | collective-permute-start | bytes 2359304 | tf_op jit(solution)/shard_map/ppermute | solution.py:19
  512.1 0.9 copy-start.12
Sparse Core Ops, SparseCore 0:
  513.1 31.7 reduce-scatter.1
where the time goes:
time: 563 us; the launch traced here: 554 us
  matrix products  226 us (40%)
  other arithmetic  127 us (23%)
  blocking collectives  86 us (15%)
  waiting for transfers between devices  56.1 us (10%)
  local copies, waits for them, and re-layouts  25.4 us (5%)
  between operations  15.3 us (3%)
  loops' own time  12.3 us (2%)
  starting transfers between devices  6 us (1%)
    dot_general x16, matrix products, cost_tile(): lax.dot_general(sources, targets, (((0,), (0,)), ((), ())), preferred_ele...  209 us
    all_gather x7, blocking collectives, joined(): everything = jax.tree.map(lambda part: lax.all_gather(part, axis), shard)  48.3 us
    reduce_sum x4, other arithmetic, row_visit(): return (block_top, jnp.sum(jnp.exp(scores - block_top[:, None]), axis=1))  35.9 us
    reduce_sum x4, other arithmetic, column_visit(): block_sum = jnp.sum(jnp.exp(scores - block_top[None, :]), axis=0)  35.7 us
    reduce_scatter x1, waiting for transfers between devices, per_device(): lax.psum_scatter(arrived, 'cell', scatter_dimension=1, tiled=True)  31.9 us
    div x2, other arithmetic, stats_visit(): weighted = plan * cost / ENTROPY  29.8 us
    psum x2, blocking collectives, per_device(): target_adj = target_push - DAMPING * lax.psum(col_part, 'cell')  29.3 us
    ppermute x2, waiting for transfers between devices, shifted(): return lax.ppermute(block, axis, route)  24.2 us
  transfers between devices with their start and end apart: 3, of which 3 were waited for; matrix products, arithmetic and copies ran while one was open for 1% of the time, Pallas kernels for 0%

commit v1 on v0

v1 whole, which is shorter than its diff:
```python
import functools

import jax
import jax.numpy as jnp
from jax import lax
from jax.experimental import pallas as pl
from jax.experimental.pallas import tpu as pltpu
from jax.sharding import PartitionSpec as P

ENTROPY = 0.25
PENALTY = 5.0
DAMPING = PENALTY / (PENALTY + ENTROPY)
MASKED = -1e30
SQ_SCALE = 1.0 / ENTROPY
DOT_SCALE = 2.0 / ENTROPY
TINY = 1e-37
SHIFT = 44.0
LOWEST = 1e-24

ROWS = 256
COLS = 512
LANES = 128
DEPTH = 128
F32 = jnp.float32
BF16 = jnp.bfloat16


def split3(value):
    high = value.astype(BF16).astype(F32)
    rest = value - high
    middle = rest.astype(BF16).astype(F32)
    return high, middle, rest - middle


def write_augmented(out_ref, start, feats, pot, is_row):
    n = feats.shape[1]
    cols = pl.ds(start, n)
    scaled = feats.astype(F32) * DOT_SCALE if is_row else feats
    out_ref[0:32, cols] = scaled.astype(out_ref.dtype)
    first = 0 if is_row else 3
    ones_from = 3 if is_row else 0
    row = lax.broadcasted_iota(jnp.int32, (16, n), 0)
    tail = jnp.where((row >= ones_from) & (row < ones_from + 3), 1.0, 0.0)
    for k, piece in enumerate(split3(pot)):
        tail = jnp.where(row == first + k, piece, tail)
    out_ref[32:48, cols] = tail.astype(out_ref.dtype)
    out_ref[48:128, cols] = jnp.zeros((80, n), out_ref.dtype)


def square_sum(feats):
    wide = feats.astype(F32)
    return jnp.sum(wide * wide, axis=0, keepdims=True)


def live_pot(feats, start, count):
    ids = start + lax.broadcasted_iota(jnp.int32, (1, feats.shape[1]), 1)
    return jnp.where(ids < count, -SQ_SCALE * square_sum(feats), MASKED)


def aligned(index, size):
    return pl.multiple_of(index * size, size)


def around(counts):
    size = counts.shape[0]
    time, member = lax.axis_index("tm"), lax.axis_index("cell")
    before = jnp.where(time > 0, counts[jnp.maximum(time - 1, 0)], 0)
    after = jnp.where(time + 1 < size, counts[jnp.minimum(time + 1, size - 1)], 0)
    return before, counts[time], after, member


def row_steps(count_here, count_next, member, group):
    blocks = pl.cdiv(count_here, LANES)
    mine = jnp.maximum((blocks - member + group - 1) // group, 0)
    per_step = ROWS // LANES
    steps = (mine + per_step - 1) // per_step
    return jnp.where(count_next > 0, steps, 0)


def col_steps(count):
    return (count + COLS - 1) // COLS


LTS = COLS // LANES
SUB = 32
WIDE = 1536


def scores(xa, ya_ref, c, cols=COLS):
    return jnp.dot(xa, ya_ref[:, pl.ds(aligned(c, cols), cols)], preferred_element_type=F32)


def piped(count, matmul, work, first_ref, second_ref, load=None, store=None):
    load = load or (lambda c: None)
    store = store or (lambda c, state: None)
    first_ref[...] = matmul(0)

    def pair(i, _):
        here, there = 2 * i, 2 * i + 1
        states = load(here), load(there)
        second_ref[...] = matmul(there)
        one = work(here, first_ref, states[0])
        first_ref[...] = matmul(jnp.minimum(there + 1, count - 1))
        two = work(there, second_ref, states[1])
        store(here, one)
        store(there, two)
        return 0

    lax.fori_loop(0, count // 2, pair, 0)

    @pl.when(count % 2 == 1)
    def _():
        store(count - 1, work(count - 1, first_ref, load(count - 1)))


def adder(acc_refs):
    def store(c, sums):
        for k, acc_ref in enumerate(acc_refs):
            lts = len(sums[k])
            for lt in range(lts):
                acc_ref[:, lane_tile(c, lt, lts)] += sums[k][lt]

    return store


def lane_tile(c, lt, lts=LTS):
    return pl.ds(aligned(c * lts + lt, LANES), LANES)


def piece_of(z_ref, rg, lt, size=SUB):
    return z_ref[rg : rg + size, lt * LANES : (lt + 1) * LANES]


def in_steps(total, visit):
    for start in range(0, total, WIDE):
        visit(start, slice(start, start + WIDE))


def kernel_a(
    counts, x0, x1, x2, x3, y0, y1, y2, y3,
    xg_ref, yg_ref, xa_ref, gb_ref, log_ref,
    ya_ref, xat_ref, za_ref, zb_ref, top_ref, sum_ref,
):
    _, count_here, count_next, member = around(counts)
    group = 4
    nb = row_steps(count_here, count_next, member, group)
    nc = col_steps(count_next)
    local = x0.shape[1]
    for k, (x_ref, y_ref) in enumerate(((x0, y0), (x1, y1), (x2, y2), (x3, y3))):
        place = pl.ds(aligned(member ^ k, local), local)
        xg_ref[:, place] = x_ref[...]
        yg_ref[:, place] = y_ref[...]
    for k in range(local // LANES):
        block_id = group * k + member
        piece = xg_ref[:, pl.ds(aligned(block_id, LANES), LANES)]
        pot = live_pot(piece, block_id * LANES, count_here) + SHIFT
        write_augmented(xat_ref, k * LANES, piece, pot, True)
        xa_ref[k * LANES : (k + 1) * LANES, :] = jnp.transpose(
            xat_ref[:, k * LANES : (k + 1) * LANES]
        ).astype(BF16)
    sum_ref[...] = jnp.zeros_like(sum_ref)

    def prepare(start, cols):
        feats = yg_ref[:, cols]
        pot = live_pot(feats, start, count_next)
        gb_ref[:, cols] = pot
        write_augmented(ya_ref, start, feats, pot, False)

    in_steps(group * local, prepare)

    def exact():
        top_ref[...] = jnp.full(top_ref.shape, MASKED, F32)
        sum_ref[...] = jnp.zeros_like(sum_ref)

        def row_visit(b, _):
            xa = xa_ref[pl.ds(aligned(b, ROWS), ROWS), :]

            def load(c):
                return [(top_ref[:, lane_tile(c, lt)], sum_ref[:, lane_tile(c, lt)]) for lt in range(LTS)]

            def work(c, z_ref, state):
                after = []
                for lt, (old, total) in enumerate(state):
                    tile = z_ref[:, lt * LANES : (lt + 1) * LANES].reshape(ROWS // 8, 8, LANES)
                    top = jnp.maximum(old, jnp.max(tile, axis=0))
                    total = total * jnp.exp(old - top) + jnp.sum(jnp.exp(tile - top[None]), axis=0)
                    after.append((top, total))
                return after

            def store(c, state):
                for lt, (top, total) in enumerate(state):
                    top_ref[:, lane_tile(c, lt)] = top
                    sum_ref[:, lane_tile(c, lt)] = total

            piped(nc, lambda c: scores(xa, ya_ref, c), work, za_ref, zb_ref, load, store)
            return 0

        lax.fori_loop(0, nb, row_visit, 0)
        tops = top_ref[...]
        top = jnp.max(tops, axis=0, keepdims=True)
        total = jnp.sum(sum_ref[...] * jnp.exp(tops - top), axis=0, keepdims=True)
        log_ref[...] = top + jnp.log(jnp.maximum(total, TINY)) - SHIFT

    thin = 2 * LANES

    def quick_visit(b, _):
        halves = [xa_ref[pl.ds(aligned(2 * b + k, ROWS // 2), ROWS // 2), :] for k in range(2)]

        def tile_sums(c, tiles):
            for t in range(tiles):
                totals = [jnp.zeros((8, LANES), F32) for _ in range(2)]
                for half in halves:
                    z = scores(half, ya_ref, c * tiles + t, thin)
                    for lt in range(2):
                        p = jnp.exp(z[:, lt * LANES : (lt + 1) * LANES])
                        totals[lt] = totals[lt] + jnp.sum(p.reshape(ROWS // 16, 8, LANES), axis=0)
                for lt in range(2):
                    sum_ref[:, lane_tile(c * tiles + t, lt, 2)] += totals[lt]

        def pair(i, _):
            tile_sums(i, 4)
            return 0

        lax.fori_loop(0, nc // 2, pair, 0)

        @pl.when(nc % 2 == 1)
        def _():
            tile_sums(nc - 1, 2)

        return 0

    lax.fori_loop(0, nb, quick_visit, 0)
    total = jnp.sum(sum_ref[...], axis=0, keepdims=True)
    log_ref[...] = jnp.where(total > 0.0, jnp.log(jnp.maximum(total, TINY)) - SHIFT, MASKED)
    ids = lax.broadcasted_iota(jnp.int32, total.shape, 1)
    lowest = jnp.min(jnp.where(ids < count_next, total, 1.0))

    @pl.when((lowest < LOWEST) & (nb > 0))
    def _():
        exact()


def column_sums(c, z_ref, _):
    rows, cols = z_ref.shape
    sums = []
    for lt in range(cols // LANES):
        p = jnp.exp(z_ref[:, lt * LANES : (lt + 1) * LANES])
        sums.append(jnp.sum(p.reshape(rows // 8, 8, LANES), axis=0))
    return [sums]


def row_adder(sum_ref, push_ref=None, g_ref=None):
    def first(c, z_ref, kept):
        for rg in range(0, ROWS, SUB):
            rows = slice(rg, rg + SUB)
            total = sum_ref[rows, :]
            push = push_ref[rows, :] if push_ref is not None else None
            for lt in range(LTS):
                z = piece_of(z_ref, rg, lt)
                p = jnp.exp(z)
                total = total + p
                kept[0][rows, lane_tile(c, lt)] = p.astype(kept[0].dtype)
                if push is not None:
                    part = p * (g_ref[:, lane_tile(c, lt)] - z)
                    push = push + part
                    kept[1][rows, lane_tile(c, lt)] = part.astype(kept[1].dtype)
            sum_ref[rows, :] = total
            if push is not None:
                push_ref[rows, :] = push

    return first


def column_parts(c, plan):
    sums = [[jnp.zeros((8, LANES), F32) for _ in range(LTS)] for _ in plan]
    for rg in range(0, ROWS, 8):
        for k, (kept_ref, weight_ref) in enumerate(plan):
            scale = weight_ref[rg : rg + 8, :]
            for lt in range(LTS):
                sums[k][lt] = sums[k][lt] + scale * kept_ref[rg : rg + 8, lane_tile(c, lt)]
    return sums


def two_stage(nb, nc, first, finish, second, store, matmul_of, buffers, kept):
    def stage(b, now, before):
        matmul = matmul_of(b)

        def work(c, z_ref, _):
            first(c, z_ref, now)
            return second(c, before) if before else None

        piped(nc, matmul, work, *buffers, store=store if before else None)
        finish(b)

    def tail(before):
        def pair(i, _):
            one, two = second(2 * i, before), second(2 * i + 1, before)
            store(2 * i, one)
            store(2 * i + 1, two)
            return 0

        lax.fori_loop(0, nc // 2, pair, 0)

        @pl.when(nc % 2 == 1)
        def _():
            store(nc - 1, second(nc - 1, before))

    even, odd = kept

    @pl.when(nb > 0)
    def _():
        stage(0, even, None)

    def visit(b, _):
        @pl.when(b % 2 == 1)
        def _():
            stage(b, odd, even)

        @pl.when(b % 2 == 0)
        def _():
            stage(b, even, odd)

        return 0

    lax.fori_loop(1, nb, visit, 0)

    @pl.when((nb > 0) & (nb % 2 == 1))
    def _():
        tail(even)

    @pl.when((nb > 0) & (nb % 2 == 0))
    def _():
        tail(odd)


def col_tile(c):
    return pl.ds(aligned(c, COLS), COLS)


def split2(value):
    high = value.astype(BF16).astype(F32)
    return high, value - high


def turned_weights(columns):
    lane = lax.broadcasted_iota(jnp.int32, (ROWS, LANES), 1)
    packed = jnp.zeros((ROWS, LANES), F32)
    for at, column in columns:
        packed = jnp.where(lane == at, column, packed)
    return jnp.transpose(packed)


def sweep(quick, exact, low_ref, lost=None):
    low_ref[...] = jnp.ones_like(low_ref)
    quick()
    again = jnp.min(low_ref[...]) < LOWEST
    if lost is not None:
        again = again | lost()

    @pl.when(again)
    def _():
        exact()


def row_lse(xa, ya_ref, nc, buffers, top_ref, sum_ref, push_ref=None, g_ref=None):
    top_ref[...] = jnp.full(top_ref.shape, MASKED, F32)
    sum_ref[...] = jnp.zeros_like(sum_ref)
    if push_ref is not None:
        push_ref[...] = jnp.zeros_like(push_ref)

    def work(c, z_ref, _):
        for rg in range(0, ROWS, SUB):
            rows = slice(rg, rg + SUB)
            old = top_ref[rows, :]
            pieces = [piece_of(z_ref, rg, lt) for lt in range(LTS)]
            top = old
            for z in pieces:
                top = jnp.maximum(top, z)
            fade = jnp.exp(old - top)
            total = sum_ref[rows, :] * fade
            push = push_ref[rows, :] * fade if push_ref is not None else None
            for lt, z in enumerate(pieces):
                p = jnp.exp(z - top)
                total = total + p
                if push is not None:
                    push = push + p * (g_ref[:, lane_tile(c, lt)] - z)
            top_ref[rows, :] = top
            sum_ref[rows, :] = total
            if push is not None:
                push_ref[rows, :] = push

    piped(nc, lambda c: scores(xa, ya_ref, c), work, *buffers)
    tops = top_ref[...]
    top = jnp.max(tops, axis=1, keepdims=True)
    fade = jnp.exp(tops - top)
    total = jnp.sum(sum_ref[...] * fade, axis=1, keepdims=True)
    if push_ref is None:
        return top, total
    return top, total, jnp.sum(push_ref[...] * fade, axis=1, keepdims=True)


def row_potential(xa):
    lane = lax.broadcasted_iota(jnp.int32, (ROWS, LANES), 1)
    wide = xa.astype(F32)
    old = jnp.sum(jnp.where((lane >= 32) & (lane < 35), wide, 0.0), axis=1, keepdims=True)
    return lane, wide, old


def with_row_potential(lane, wide, pot):
    high, middle, low = split3(pot)
    new = jnp.where(lane == 32, high, jnp.where(lane == 33, middle, jnp.where(lane == 34, low, wide)))
    return new.astype(BF16)


def kernel_b(counts, xa_ref, yg_ref, gb_ref, l0, l1, l2, l3, g_ref, col_ref, ya_ref, za_ref, zb_ref, p_ref, q_ref, top_ref, sum_ref, weight_ref, low_ref, most_ref, acc_ref):
    _, count_here, count_next, member = around(counts)
    nb = row_steps(count_here, count_next, member, 4)
    nc = col_steps(count_next)

    def prepare(start, cols):
        logs = [ref[:, cols] for ref in (l0, l1, l2, l3)]
        top = jnp.maximum(jnp.maximum(logs[0], logs[1]), jnp.maximum(logs[2], logs[3]))
        total = sum(jnp.exp(one - top) for one in logs)
        ids = start + lax.broadcasted_iota(jnp.int32, (1, WIDE), 1)
        pot = jnp.where(ids < count_next, -DAMPING * (top + jnp.log(total)), 0.0)
        g_ref[:, cols] = pot
        write_augmented(ya_ref, start, yg_ref[:, cols], pot + gb_ref[:, cols], False)

    in_steps(yg_ref.shape[1], prepare)

    buffers = za_ref, zb_ref

    def quick():
        acc_ref[...] = jnp.zeros_like(acc_ref)

        def matmul_of(b):
            sum_ref[...] = jnp.zeros_like(sum_ref)
            xa = xa_ref[pl.ds(aligned(b, ROWS), ROWS), :]
            return lambda c: scores(xa, ya_ref, c)

        def finish(b):
            lane, wide, old = row_potential(xa_ref[pl.ds(aligned(b, ROWS), ROWS), :])
            live = old > 0.5 * MASKED
            total = jnp.sum(sum_ref[...], axis=1, keepdims=True)
            low_ref[...] = jnp.minimum(low_ref[...], jnp.where(live, total, 1.0))
            pot = -DAMPING * (jnp.log(jnp.maximum(total, TINY)) - SHIFT)
            weight = jnp.where(live, jnp.exp(pot - SHIFT), 0.0)
            weight_ref[...] = jnp.broadcast_to(weight, weight_ref.shape)
            most_ref[...] = jnp.maximum(most_ref[...], weight)

        two_stage(
            nb, nc, row_adder(sum_ref), finish, lambda c, kept: column_parts(c, [(kept[0], weight_ref)]),
            adder([acc_ref]), matmul_of, buffers, ((p_ref,), (q_ref,)),
        )

    def exact():
        acc_ref[...] = jnp.zeros_like(acc_ref)

        def row_visit(b, _):
            xa = xa_ref[pl.ds(aligned(b, ROWS), ROWS), :]
            lane, wide, old = row_potential(xa)
            live = old > 0.5 * MASKED
            top, total = row_lse(xa, ya_ref, nc, buffers, top_ref, sum_ref)
            pot = -DAMPING * (top + jnp.log(total) - SHIFT)
            xb = with_row_potential(lane, wide, jnp.where(live, pot + old - SHIFT, MASKED))
            piped(nc, lambda c: scores(xb, ya_ref, c), column_sums, *buffers, store=adder([acc_ref]))
            return 0

        lax.fori_loop(0, nb, row_visit, 0)

    def lost():
        total = jnp.sum(acc_ref[...], axis=0, keepdims=True)
        ids = lax.broadcasted_iota(jnp.int32, total.shape, 1)
        least = jnp.min(jnp.where((ids < count_next) & (nb > 0), total, 1.0))
        return least < jnp.max(most_ref[...]) * 2.0**-91

    most_ref[...] = jnp.zeros_like(most_ref)
    sweep(quick, exact, low_ref, lost)
    col_ref[...] = jnp.sum(acc_ref[...], axis=0, keepdims=True)


def kernel_c(
    counts, xa_ref, yg_ref, gb_ref, g_ref, c0, c1, c2, c3,
    xb_ref, aux_ref, g2_ref, col_ref,
    ya_ref, za_ref, zb_ref, p_ref, w_ref, q_ref, v_ref, top_ref, sum_ref, push_ref, adj_ref, low_ref, cost_ref, weight_ref, acc_ref, acc0_ref, acc1_ref, acc2_ref,
):
    _, count_here, count_next, member = around(counts)
    nb = row_steps(count_here, count_next, member, 4)
    nc = col_steps(count_next)

    def prepare(start, cols):
        total = (c0[:, cols] + c1[:, cols]) + (c2[:, cols] + c3[:, cols])
        ids = start + lax.broadcasted_iota(jnp.int32, (1, WIDE), 1)
        log = jnp.log(jnp.maximum(total, TINY)) - g_ref[:, cols]
        pot = jnp.where(ids < count_next, -DAMPING * log, 0.0)
        g2_ref[:, cols] = pot
        write_augmented(ya_ref, start, yg_ref[:, cols], pot + gb_ref[:, cols], False)

    in_steps(yg_ref.shape[1], prepare)

    buffers = za_ref, zb_ref
    accs = acc0_ref, acc1_ref, acc2_ref

    ids = lax.broadcasted_iota(jnp.int32, g_ref.shape, 1)
    centre = jnp.sum(jnp.where(ids < count_next, g_ref[...], 0.0), axis=1, keepdims=True)
    centre = centre / (DAMPING * jnp.maximum(count_next, 1).astype(F32)) + 3.0
    cost_ref[...] = g2_ref[...] + (SHIFT - centre)

    def close_rows(b, top, total, push):
        rows_here = pl.ds(aligned(b, ROWS), ROWS)
        lane, wide, old = row_potential(xa_ref[rows_here, :])
        live = old > 0.5 * MASKED
        total = jnp.maximum(total, TINY)
        row_log = top + jnp.log(total) - SHIFT
        pot = jnp.where(live, -DAMPING * row_log, 0.0)
        row_sum = jnp.where(live, jnp.exp(row_log + pot), 0.0)
        adjoint = jnp.where(live, push / total + centre, 0.0)
        inverse = jnp.where(row_sum > 0.0, 1.0 / jnp.maximum(row_sum, TINY), 0.0)
        full = jnp.where(live, pot + old - SHIFT, MASKED)
        xb = with_row_potential(lane, wide, full)
        xb_ref[rows_here, :] = xb
        aux = jnp.where(lane == 0, adjoint, jnp.where(lane == 1, inverse, jnp.where(lane == 2, pot, full)))
        aux_ref[rows_here, :] = aux
        return live, pot, adjoint, xb

    def quick():
        acc_ref[...] = jnp.zeros_like(acc_ref)

        def matmul_of(b):
            sum_ref[...] = jnp.zeros_like(sum_ref)
            push_ref[...] = jnp.zeros_like(push_ref)
            xa = xa_ref[pl.ds(aligned(b, ROWS), ROWS), :]
            return lambda c: scores(xa, ya_ref, c)

        def finish(b):
            total = jnp.sum(sum_ref[...], axis=1, keepdims=True)
            push = jnp.sum(push_ref[...], axis=1, keepdims=True)
            live, pot, adjoint, _ = close_rows(b, 0.0, total, push)
            low_ref[...] = jnp.minimum(low_ref[...], jnp.where(live, total, 1.0))
            weight = jnp.where(live, jnp.exp(pot - SHIFT), 0.0)
            pieces = (*split2(weight), *split2(weight * adjoint))
            weight_ref[...] = turned_weights(list(enumerate(pieces)))[0:16, :].astype(BF16)

        def second(c, kept):
            weights = weight_ref[...]
            plan = jnp.dot(weights, kept[0][:, col_tile(c)], preferred_element_type=F32)
            cost = jnp.dot(weights, kept[1][:, col_tile(c)], preferred_element_type=F32)
            return plan, cost

        def store(c, sums):
            acc_ref[0:16, col_tile(c)] += sums[0]
            acc_ref[16:32, col_tile(c)] += sums[1]

        two_stage(
            nb, nc, row_adder(sum_ref, push_ref, cost_ref), finish, second, store, matmul_of, buffers,
            ((p_ref, w_ref), (q_ref, v_ref)),
        )
        acc0_ref[0:1, :] = acc_ref[0:1, :] + acc_ref[1:2, :]
        acc1_ref[0:1, :] = acc_ref[16:17, :] + acc_ref[17:18, :]
        acc2_ref[0:1, :] = acc_ref[2:3, :] + acc_ref[3:4, :]
        for ref in accs:
            ref[1:8, :] = jnp.zeros((7, ref.shape[1]), F32)

    def exact():
        for ref in accs:
            ref[...] = jnp.zeros_like(ref)

        def row_visit(b, _):
            xa = xa_ref[pl.ds(aligned(b, ROWS), ROWS), :]
            top, total, push = row_lse(xa, ya_ref, nc, buffers, top_ref, sum_ref, push_ref, cost_ref)
            _, pot, adjoint, xb = close_rows(b, top, total, push)
            top_ref[...] = jnp.broadcast_to(pot - SHIFT, top_ref.shape)
            adj_ref[...] = jnp.broadcast_to(adjoint, adj_ref.shape)

            def work(c, z_ref, _):
                sums = [[jnp.zeros((8, LANES), F32) for _ in range(LTS)] for _ in range(3)]
                for rg in range(0, ROWS, 8):
                    pot_here = top_ref[rg : rg + 8, :]
                    adj_here = adj_ref[rg : rg + 8, :]
                    for lt in range(LTS):
                        tile = piece_of(z_ref, rg, lt, 8)
                        p = jnp.exp(tile)
                        sums[0][lt] = sums[0][lt] + p
                        sums[1][lt] = sums[1][lt] + p * (cost_ref[:, lane_tile(c, lt)] + (pot_here - tile))
                        sums[2][lt] = sums[2][lt] + p * adj_here
                return sums

            piped(nc, lambda c: scores(xb, ya_ref, c), work, *buffers, store=adder(accs))
            return 0

        lax.fori_loop(0, nb, row_visit, 0)

    sweep(quick, exact, low_ref)
    mass = jnp.sum(acc0_ref[...], axis=0, keepdims=True)
    slots = mass.shape[1]
    col_ref[:, 0:slots] = mass
    push = jnp.sum(acc1_ref[...], axis=0, keepdims=True)
    col_ref[:, slots : 2 * slots] = push + centre * mass
    col_ref[:, 2 * slots :] = jnp.sum(acc2_ref[...], axis=0, keepdims=True)


def kernel_d(
    counts, xb_ref, aux_ref, yg_ref, gb_ref, g2_ref, s0, s1, s2, s3,
    stat_ref, send_ref,
    ya_ref, za_ref, zb_ref, p_ref, q_ref, values_ref, sum_ref, weight_ref, acc_ref,
):
    _, count_here, count_next, member = around(counts)
    nb = row_steps(count_here, count_next, member, 4)
    nc = col_steps(count_next)
    slots = yg_ref.shape[1]
    local = xb_ref.shape[0]
    acc_ref[...] = jnp.zeros_like(acc_ref)

    def prepare(start, cols):
        mass, push, pulled = (
            (s0[:, part] + s1[:, part]) + (s2[:, part] + s3[:, part])
            for part in (pl.ds(start + k * slots, WIDE) for k in range(3))
        )
        inverse = jnp.where(mass > 0.0, 1.0 / jnp.maximum(mass, TINY), 0.0)
        pot = g2_ref[:, cols]
        over, later = push * inverse, (push - DAMPING * pulled) * inverse
        stat_ref[0:1, cols] = pot + gb_ref[:, cols]
        stat_ref[1:2, cols] = over
        stat_ref[2:3, cols] = pot
        stat_ref[3:8, cols] = jnp.zeros((5, WIDE), F32)
        row = lax.broadcasted_iota(jnp.int32, (16, WIDE), 0)
        values = jnp.where(row == 0, 1.0, 0.0)
        for k, piece in enumerate((*split2(over), *split2(later))):
            values = jnp.where(row == k + 1, piece, values)
        values_ref[:, cols] = values.astype(BF16)
        write_augmented(ya_ref, start, yg_ref[:, cols], pot + gb_ref[:, cols], False)

    in_steps(slots, prepare)
    rest = 2 * slots
    send_ref[:, rest : rest + local] = jnp.full((1, local), MASKED, F32)
    send_ref[:, rest + local :] = jnp.zeros((1, local), F32)

    def matmul_of(b):
        sum_ref[...] = jnp.zeros_like(sum_ref)
        xb = xb_ref[pl.ds(aligned(b, ROWS), ROWS), :]
        return lambda c: scores(xb, ya_ref, c)

    def first(c, z_ref, kept):
        rounded = []
        for rg in range(0, ROWS, SUB):
            line = []
            for lt in range(LTS):
                p = jnp.exp(piece_of(z_ref, rg, lt)).astype(BF16)
                kept[0][rg : rg + SUB, lane_tile(c, lt)] = p
                line.append(p)
            rounded.append(jnp.concatenate(line, axis=1))
        sum_ref[...] += lax.dot_general(
            jnp.concatenate(rounded, axis=0), values_ref[:, col_tile(c)], (((1,), (1,)), ((), ())),
            preferred_element_type=F32,
        )

    def finish(b):
        sums = sum_ref[...]
        inverse = jnp.where(sums[:, 0:1] > 0.0, 1.0 / jnp.maximum(sums[:, 0:1], TINY), 0.0)
        middle, last = sums[:, 1:2] + sums[:, 2:3], sums[:, 3:4] + sums[:, 4:5]
        aux = aux_ref[pl.ds(aligned(b, ROWS), ROWS), :]
        start_adj, pot, full = aux[:, 0:1], aux[:, 2:3], aux[:, 3:4]
        middle_adj = start_adj - DAMPING * middle * inverse
        last_adj = start_adj - DAMPING * last * inverse
        alpha = 1.0 + DAMPING * last_adj - pot
        high, low = split2(middle_adj)
        packed = turned_weights([(0, full), (1, alpha), (8, jnp.ones_like(high)), (9, high), (10, low)])
        weight_ref[...] = packed[8:24, :].astype(BF16)
        send_ref[:, pl.ds(aligned(b + rest // ROWS, ROWS), ROWS)] = packed[0:1, :]
        send_ref[:, pl.ds(aligned(b + (rest + local) // ROWS, ROWS), ROWS)] = packed[1:2, :]

    def second(c, kept):
        return jnp.dot(weight_ref[...], kept[0][:, col_tile(c)], preferred_element_type=F32)

    def store(c, sums):
        acc_ref[:, col_tile(c)] += sums

    two_stage(
        nb, nc, first, finish, second, store, matmul_of, (za_ref, zb_ref), ((p_ref,), (q_ref,)),
    )
    send_ref[:, 0:slots] = acc_ref[0:1, :]
    send_ref[:, slots:rest] = acc_ref[1:2, :] + acc_ref[2:3, :]


def kernel_f(counts, p0, p1, p2, p3, stat_ref, col_ref, mine_ref, early_ref, parts_ref):
    member = lax.axis_index("cell")
    slots, local = stat_ref.shape[1], mine_ref.shape[1]
    for k, ref in enumerate((p0, p1, p2, p3)):
        parts_ref[member ^ k] = ref[...]
    mass, total = (
        (p0[:, part] + p1[:, part]) + (p2[:, part] + p3[:, part]) for part in (slice(0, slots), slice(slots, 2 * slots))
    )
    inverse = jnp.where(mass > 0.0, 1.0 / jnp.maximum(mass, TINY), 0.0)
    last = stat_ref[1:2, :] - DAMPING * total * inverse
    col_ref[0:1, :] = stat_ref[0:1, :]
    col_ref[1:2, :] = DAMPING * last - stat_ref[2:3, :]
    for block in range(slots // LANES):
        owner, place = block % 4, block // 4
        lanes = slice(block * LANES, (block + 1) * LANES)
        for k in range(2):
            at = 2 * slots + k * local + place * LANES
            early_ref[k : k + 1, lanes] = parts_ref[owner, :, at : at + LANES]
    here = pl.ds(aligned(member, local), local)
    mine_ref[...] = early_ref[:, here]
    early_ref[:, slots:] = col_ref[:, here]


def kernel_e(
    counts, *refs, earlier,
):
    own_ref, rowpot_ref, other_ref, colpot_ref = refs[:4]
    base_ref = refs[4] if earlier else None
    out_ref, xw_ref, tile_ref, ys_ref, beta_ref, za_ref, zb_ref, pull_ref, sum_ref = refs[5 if earlier else 4 :]
    local, slots = own_ref.shape[1], other_ref.shape[1]
    before, here, after, member = around(counts)
    count_rows = jnp.clip(here - member * local, 0, local)
    count_cols = before if earlier else after
    if earlier:
        own_at = slots
    else:
        own_at = 0
    nc = col_steps(count_cols)
    nb = jnp.where(count_cols > 0, (count_rows + ROWS - 1) // ROWS, 0)
    out_ref[...] = base_ref[...] if earlier else jnp.zeros_like(out_ref)

    def prepare(c, _):
        cols = pl.ds(aligned(c, COLS), COLS)
        write_augmented(tile_ref, 0, other_ref[:, cols], colpot_ref[0:1, cols], False)
        ys_ref[cols, :] = jnp.transpose(tile_ref[...]).astype(BF16)
        beta_ref[cols, :] = jnp.transpose(jnp.broadcast_to(colpot_ref[1:2, cols], (LANES, COLS)))
        return 0

    @pl.when(nb > 0)
    def _():
        lax.fori_loop(0, nc, prepare, 0)

    def row_visit(b, _):
        rows_here = pl.ds(aligned(b, ROWS), ROWS)
        own = own_ref[:, rows_here]
        own_pots = pl.ds(aligned(b + own_at // ROWS, ROWS), ROWS)
        write_augmented(xw_ref, 0, own, rowpot_ref[0:1, own_pots], True)
        xw = xw_ref[...]
        alpha = rowpot_ref[1:2, own_pots]
        sum_ref[...] = jnp.zeros_like(sum_ref)
        pull_ref[...] = jnp.zeros_like(pull_ref)

        def matmul(c):
            return jnp.dot(ys_ref[pl.ds(aligned(c, COLS), COLS), :], xw, preferred_element_type=F32)

        def work(c, z_ref, _):
            rounded = []
            sums = [jnp.zeros((8, LANES), F32) for _ in range(ROWS // LANES)]
            for jg in range(0, COLS, 16):
                beta = beta_ref[pl.ds(pl.multiple_of(c * COLS + jg, 16), 16), :]
                line = []
                for lt in range(ROWS // LANES):
                    tile = piece_of(z_ref, jg, lt, 16)
                    grad = jnp.exp(tile) * (tile + (alpha[:, lt * LANES : (lt + 1) * LANES] + beta))
                    sums[lt] = sums[lt] + (grad[0:8] + grad[8:16])
                    line.append(grad.astype(BF16))
                rounded.append(jnp.concatenate(line, axis=1))
            for lt in range(ROWS // LANES):
                sum_ref[:, lt * LANES : (lt + 1) * LANES] += sums[lt]
            feats = other_ref[:, pl.ds(aligned(c, COLS), COLS)]
            pull_ref[...] += jnp.dot(feats, jnp.concatenate(rounded, axis=0), preferred_element_type=F32)

        piped(nc, matmul, work, za_ref, zb_ref)
        total = jnp.sum(sum_ref[...], axis=0, keepdims=True)
        out_ref[:, rows_here] += 2.0 * (own.astype(F32) * total - pull_ref[...])
        return 0

    lax.fori_loop(0, nb, row_visit, 0)


def run(body, name, outs, scratch, limit, counts, *operands, flops=0):
    vmem = pl.BlockSpec(memory_space=pltpu.VMEM)
    return pl.pallas_call(
        body,
        name=name,
        out_shape=outs,
        in_specs=[pl.BlockSpec(memory_space=pltpu.SMEM)] + [vmem] * len(operands),
        out_specs=jax.tree.map(lambda _: vmem, outs),
        scratch_shapes=scratch,
        compiler_params=pltpu.CompilerParams(vmem_limit_bytes=limit * 1024 * 1024),
        cost_estimate=pl.CostEstimate(flops=flops, bytes_accessed=4_000_000, transcendentals=9_000_000),
    )(counts, *operands)


def shape(*dims, dtype=F32):
    return jax.ShapeDtypeStruct(dims, dtype)


def shifted(block, distance):
    size = lax.axis_size("tm")
    route = [(i - distance, i) for i in range(size) if 0 <= i - distance < size]
    return lax.ppermute(block, "tm", route)


def swapped(block, k):
    return lax.ppermute(block, "cell", [(i, i ^ k) for i in range(lax.axis_size("cell"))])


def exchanged(block):
    near = swapped(block, 1)
    far = swapped(block, 2)
    return [block, near, far, swapped(far, 1)]


def per_device(embedding, counts):
    feat_dim, local = embedding.shape
    group = lax.axis_size("cell")
    slots = local * group

    target_parts = exchanged(shifted(embedding, -1))
    source_parts = exchanged(embedding)

    flops = 2 * local * slots * DEPTH
    aug = pltpu.VMEM((DEPTH, slots), BF16)
    narrow = pltpu.VMEM((ROWS, LANES), F32)
    wide = pltpu.VMEM((ROWS, slots), F32)
    half = pltpu.VMEM((ROWS, slots), BF16)
    turned_rows = pltpu.VMEM((16, ROWS), BF16)
    buffers = [pltpu.VMEM((ROWS, COLS), F32)] * 2
    long = pltpu.VMEM((8, slots), F32)
    grouped, targets, xa, gb, log = run(
        kernel_a, "column_log",
        (
            shape(feat_dim, slots, dtype=BF16), shape(feat_dim, slots, dtype=BF16),
            shape(local, DEPTH, dtype=BF16), shape(1, slots), shape(1, slots),
        ),
        [aug, pltpu.VMEM((DEPTH, local), F32), *buffers, long, long],
        16, counts, *source_parts, *target_parts, flops=flops,
    )
    logs = exchanged(log)
    g1, col1 = run(
        kernel_b, "first_sweep",
        (shape(1, slots), shape(1, slots)),
        [aug, *buffers, wide, wide, narrow, narrow, narrow, narrow, narrow, long],
        24, counts, xa, targets, gb, *logs, flops=2 * flops,
    )
    grouped, col1 = lax.optimization_barrier((grouped, col1))
    earlier = shifted(grouped, 1)
    xb, aux, g2, stats = run(
        kernel_c, "second_sweep",
        (shape(local, DEPTH, dtype=BF16), shape(local, LANES), shape(1, slots), shape(1, 3 * slots)),
        [
            aug, *buffers, half, half, half, half, narrow, narrow, narrow, narrow, narrow,
            pltpu.VMEM((1, slots), F32), turned_rows, pltpu.VMEM((32, slots), F32), long, long, long,
        ],
        28, counts, xa, targets, gb, g1, *exchanged(col1), flops=2 * flops,
    )
    xb, earlier = lax.optimization_barrier((xb, earlier))
    stat, send = run(
        kernel_d, "adjoint",
        (shape(8, slots), shape(1, 2 * slots + 2 * local)),
        [
            aug, *buffers, half, half, pltpu.VMEM((16, slots), BF16), pltpu.VMEM((ROWS, 16), F32), turned_rows,
            pltpu.VMEM((16, slots), F32),
        ],
        20, counts, xb, aux, targets, gb, g2, *exchanged(stats), flops=2 * flops,
    )
    col_pair, rows_mine, early = run(
        kernel_f, "assemble",
        (shape(2, slots), shape(2, local), shape(2, slots + local)),
        [pltpu.VMEM((group, 1, 2 * slots + 2 * local), F32)],
        8, counts, *exchanged(send), stat,
    )
    early = shifted(early, 1)

    turned = [pltpu.VMEM((COLS, ROWS), F32)] * 2
    scratch_e = [
        pltpu.VMEM((DEPTH, ROWS), BF16), pltpu.VMEM((DEPTH, COLS), F32), pltpu.VMEM((slots, DEPTH), BF16),
        pltpu.VMEM((slots, LANES), F32), *turned, pltpu.VMEM((feat_dim, ROWS), F32), pltpu.VMEM((8, ROWS), F32),
    ]
    source_grad = run(
        functools.partial(kernel_e, earlier=False), "source_gradient", shape(feat_dim, local), scratch_e,
        16, counts, embedding, rows_mine, targets, col_pair, flops=2 * flops,
    )
    return run(
        functools.partial(kernel_e, earlier=True), "target_gradient", shape(feat_dim, local), scratch_e,
        16, counts, embedding, early, earlier, early, source_grad, flops=2 * flops,
    )


def solution(mesh):
    in_specs = (P(None, ("tm", "cell")), P())
    out_specs = P(None, ("tm", "cell"))
    return jax.shard_map(
        per_device, mesh=mesh, in_specs=in_specs, out_specs=out_specs, check_vma=False
    )
```

time: 563 us -> 144 us (0.26); the launches traced: 554 us -> 143 us
  matrix products: 226 us -> 0 us
  other arithmetic: 127 us -> 0 us
  Pallas kernels: 0 us -> 95.7 us
  blocking collectives: 86 us -> 0 us
  waiting for transfers between devices: 56.1 us -> 29.6 us
  local copies, waits for them, and re-layouts: 25.4 us -> 2.21 us
  between operations: 15.3 us -> 0.18 us
  loops' own time: 12.3 us -> 0 us
  starting transfers between devices: 6 us -> 15.2 us
    dot_general x20 -> x0, matrix products: 226 us -> none  [the longest x16 209 us: cost_tile(): lax.dot_general(sources, targets, (((0,), (0,)), ((), ())), preferred_ele...]
    pallas_call x0 -> x7, Pallas kernels: none -> 95.7 us  [run(): pl.pallas_call(body, name=name, out_shape=outs, in_specs=[pl.BlockSpec(me...]
    reduce_sum x12 -> x0, other arithmetic: 91.2 us -> none  [the longest x4 35.9 us: row_visit(): return (block_top, jnp.sum(jnp.exp(scores - block_top[:, None]), axis=1))]
    all_gather x8 -> x0, blocking collectives: 56.7 us -> none  [the longest x7 48.3 us: joined(): everything = jax.tree.map(lambda part: lax.all_gather(part, axis), shard)]
    reduce_scatter x1 -> x0, waiting for transfers between devices: 31.9 us -> none  [per_device(): lax.psum_scatter(arrived, 'cell', scatter_dimension=1, tiled=True)]
    div x2 -> x0, other arithmetic: 29.8 us -> none  [stats_visit(): weighted = plan * cost / ENTROPY]
    psum x2 -> x0, blocking collectives: 29.3 us -> none  [per_device(): target_adj = target_push - DAMPING * lax.psum(col_part, 'cell')]
    dynamic_slice x83 -> x0, local copies, waits for them, and re-layouts: 16.1 us -> none  [the longest x16 9.94 us: per_device(): result, _ = lax.scan(column_visit, (masked_cols, zero_cols), block_ids)]
  transfers between devices with their start and end apart: 3 -> 21, of which waited for: 3 -> 11; matrix products, arithmetic and copies ran while one was open for 1% -> 0% of each run, Pallas kernels for 0% -> 26%
where the time goes in v1:
time: 144 us; the launch traced here: 143 us
  Pallas kernels  95.7 us (66%)
  waiting for transfers between devices  29.6 us (21%)
  starting transfers between devices  15.2 us (11%)
  local copies, waits for them, and re-layouts  2.21 us (2%)
    pallas_call x7, Pallas kernels, run(): pl.pallas_call(body, name=name, out_shape=outs, in_specs=[pl.BlockSpec(me...  95.7 us
    ppermute x18, waiting for transfers between devices, swapped(): lax.ppermute(block, 'cell', [(i, i ^ k) for i in range(lax.axis_size('cel...  28.9 us
    ppermute x18, starting transfers between devices, swapped(): lax.ppermute(block, 'cell', [(i, i ^ k) for i in range(lax.axis_size('cel...  8.36 us
    ppermute x3, starting transfers between devices, shifted(): return lax.ppermute(block, 'tm', route)  6.85 us
  transfers between devices with their start and end apart: 21, of which 11 were waited for; matrix products, arithmetic and copies ran while one was open for 0% of the time, Pallas kernels for 26%

profile of v1, /device:TPU:68, one launch (start us, length us, event | category | flops | bytes accessed | tf_op | source)
XLA Modules:
  0.0 142.9 jit_solution(14551855348249282612)
XLA Ops:
  0.0 3.0 %collective-permute-start.3 = (bf16[32,1536]{1,0:T(8,128)(2,1)}, bf16[32,1536]{1,0:T(8,128)(2,1)S(1)}, u32[]{:S(2)}, u32[]{:S(2)}) collective-permute-start(bf16[32,1536]{1,0:T(8,128)(2,1)} %refs_0_.3), channel_id=1, source_target_pairs={{4,0},{8,4},{12,8},{16,12},{20,16},{24,20},{28,24},{32,28},{36,32}... | collective-permute-start | bytes 294920 | tf_op jit(solution)/shard_map/ppermute | solution.py:796
  3.0 3.0 %collective-permute-start.1 = (bf16[32,1536]{1,0:T(8,128)(2,1)}, bf16[32,1536]{1,0:T(8,128)(2,1)S(1)}, u32[]{:S(2)}, u32[]{:S(2)}) collective-permute-start(bf16[32,1536]{1,0:T(8,128)(2,1)} %refs_0_.3), channel_id=1, source_target_pairs={{0,2},{1,3},{2,0},{3,1},{4,6},{5,7},{6,4},{7,5},{8,10},{9,11},{10,... | collective-permute-start | bytes 294920 | tf_op jit(solution)/shard_map/ppermute | solution.py:800
  6.0 0.7 collective-permute-done.3.y0
  6.7 4.2 %collective-permute-start.5 = (bf16[32,1536]{1,0:T(8,128)(2,1)S(1)}, bf16[32,1536]{1,0:T(8,128)(2,1)S(1)}, u32[]{:S(2)}, u32[]{:S(2)}) collective-permute-start(bf16[32,1536]{1,0:T(8,128)(2,1)S(1)} %collective-permute-done.3.y0), channel_id=1, source_target_pairs={{0,2},{1,3},{2,0},{3,1},{4,6},{5,7},{6,4},{7,5},{8,10},{9,11},{10,... | collective-permute-start | bytes 294920 | tf_op jit(solution)/shard_map/ppermute | solution.py:800
  10.9 0.0 collective-permute-start
  10.9 0.5 collective-permute-start.4
  11.4 0.4 collective-permute-done.1.x2
  11.8 0.0 collective-permute-start.2
  11.8 1.7 %collective-permute-done.5.y2 = bf16[32,1536]{1,0:T(8,128)(2,1)S(1)} collective-permute-done((bf16[32,1536]{1,0:T(8,128)(2,1)S(1)}, bf16[32,1536]{1,0:T(8,128)(2,1)S(1)}, u32[]{:S(2)}, u32[]{:S(2)}) %collective-permute-start.5) | collective-permute-done | bytes 98336 | tf_op jit(solution)/shard_map/ppermute | solution.py:800
  13.5 0.0 collective-permute-start.6
  13.5 0.0 collective-permute-done.x1
  13.5 0.0 collective-permute-done.4.y1
  13.5 0.0 collective-permute-done.2.x3
  13.5 1.3 collective-permute-done.6.y3
  14.8 0.9 copy-done
  15.7 0.7 copy-done.2
  16.3 19.7 %column_log.1 = (bf16[32,6144]{1,0:T(8,128)(2,1)S(1)}, bf16[32,6144]{1,0:T(8,128)(2,1)S(1)}, bf16[1536,128]{1,0:T(8,128)(2,1)S(1)}, f32[1,6144]{1,0:T(1,128)S(1)}, f32[1,6144]{1,0:T(1,128)S(1)}) custom-call(s32[32]{0:T(128)S(1)} %copy-done.2, bf16[32,1536]{1,0:T(8,128)(2,1)S(1)} %copy-done, bf16[32,1536]{1,0:T(8,128)(2,1)S(1)} %collective-permute-done.x1, ...), custom_call_target="tpu_custom_call" | custom-call | flops 2415919104 | bytes 4000000 | tf_op jit(solution)/shard_map/column_log/pallas_call | solution.py:777
  36.0 0.1 collective-permute-start.8
  36.1 0.1 collective-permute-start.7
  36.2 5.2 %collective-permute-done.8.l2 = f32[1,6144]{1,0:T(1,128)S(1)} collective-permute-done((f32[1,6144]{1,0:T(1,128)S(1)}, f32[1,6144]{1,0:T(1,128)S(1)}, u32[]{:S(2)}, u32[]{:S(2)}) %collective-permute-start.8) | collective-permute-done | bytes 24608 | tf_op jit(solution)/shard_map/ppermute | solution.py:800
  41.4 0.0 collective-permute-start.9
  41.4 0.0 collective-permute-done.7.l1
  41.4 1.2 collective-permute-done.9.l3
  42.6 0.7 copy-done.3
  43.3 13.0 %first_sweep.1 = (f32[1,6144]{1,0:T(1,128)S(1)}, f32[1,6144]{1,0:T(1,128)S(1)}) custom-call(s32[32]{0:T(128)S(1)} %copy-done.3, bf16[1536,128]{1,0:T(8,128)(2,1)S(1)} %get-tuple-element.25.xa_ref, bf16[32,6144]{1,0:T(8,128)(2,1)S(1)} %get-tuple-element.26.yg_ref.refs_2_, f32[1,6144]{1,0:T(1,128)S(1)} %get-tuple-element.27.gb_ref, ...), custom_call_target="tpu_custom_call" | custom-call | flops 4831838208 | bytes 4000000 | tf_op jit(solution)/shard_map/first_sweep/pallas_call | solution.py:777
  56.3 0.1 collective-permute-start.11
  56.4 0.1 collective-permute-start.10
  56.5 5.2 %collective-permute-done.11.c2 = f32[1,6144]{1,0:T(1,128)S(1)} collective-permute-done((f32[1,6144]{1,0:T(1,128)S(1)}, f32[1,6144]{1,0:T(1,128)S(1)}, u32[]{:S(2)}, u32[]{:S(2)}) %collective-permute-start.11) | collective-permute-done | bytes 24608 | tf_op jit(solution)/shard_map/ppermute | solution.py:800
  61.7 0.0 collective-permute-start.12
  61.7 1.9 %collective-permute-start.13 = (bf16[32,6144]{1,0:T(8,128)(2,1)S(1)}, bf16[32,6144]{1,0:T(8,128)(2,1)S(1)}, u32[]{:S(2)}, u32[]{:S(2)}) collective-permute-start(bf16[32,6144]{1,0:T(8,128)(2,1)S(1)} %get-tuple-element.34), channel_id=1, source_target_pairs={{0,4},{4,8},{8,12},{12,16},{16,20},{20,24},{24,28},{28,32},{32,36}... | collective-permute-start | bytes 1179656 | tf_op jit(solution)/shard_map/ppermute | solution.py:796
  63.6 0.0 collective-permute-done.12.c3
  63.7 17.9 %second_sweep.1 = (bf16[1536,128]{1,0:T(8,128)(2,1)S(1)}, f32[1536,128]{1,0:T(8,128)S(1)}, f32[1,6144]{1,0:T(1,128)S(1)}, f32[1,18432]{1,0:T(1,128)S(1)}) custom-call(s32[32]{0:T(128)S(1)} %copy-done.3, bf16[1536,128]{1,0:T(8,128)(2,1)S(1)} %get-tuple-element.25.xa_ref, bf16[32,6144]{1,0:T(8,128)(2,1)S(1)} %get-tuple-element.26.yg_ref.refs_2_, ...), custom_call_target="tpu_custom_call" | custom-call | flops 4831838208 | bytes 4000000 | tf_op jit(solution)/shard_map/second_sweep/pallas_call | solution.py:777
  81.5 0.1 collective-permute-start.15
  81.6 0.1 collective-permute-start.14
  81.7 5.8 %collective-permute-done.15.s2 = f32[1,18432]{1,0:T(1,128)S(1)} collective-permute-done((f32[1,18432]{1,0:T(1,128)S(1)}, f32[1,18432]{1,0:T(1,128)S(1)}, u32[]{:S(2)}, u32[]{:S(2)}) %collective-permute-start.15) | collective-permute-done | bytes 73760 | tf_op jit(solution)/shard_map/ppermute | solution.py:800
  87.5 0.0 collective-permute-done.13.refs_2_
  87.5 0.0 collective-permute-done.14.s1
  87.5 1.3 collective-permute-done.16.s3
  88.7 17.7 %adjoint.1 = (f32[8,6144]{1,0:T(8,128)S(1)}, f32[1,15360]{1,0:T(1,128)S(1)}) custom-call(s32[32]{0:T(128)S(1)} %copy-done.3, bf16[1536,128]{1,0:T(8,128)(2,1)S(1)} %get-tuple-element.35.xb_ref, f32[1536,128]{1,0:T(8,128)S(1)} %get-tuple-element.36.aux_ref, bf16[32,6144]{1,0:T(8,128)(2,1)S(1)} %get-tuple-element.26.yg_ref.refs_2_, ...), custom_call_target="tpu_custom_call" | custom-call | flops 4831838208 | bytes 4000000 | tf_op jit(solution)/shard_map/adjoint/pallas_call | solution.py:777
  106.4 0.1 collective-permute-start.18
  106.5 0.1 collective-permute-start.17
  106.6 5.6 %collective-permute-done.18.p2 = f32[1,15360]{1,0:T(1,128)S(1)} collective-permute-done((f32[1,15360]{1,0:T(1,128)S(1)}, f32[1,15360]{1,0:T(1,128)S(1)}, u32[]{:S(2)}, u32[]{:S(2)}) %collective-permute-start.18) | collective-permute-done | bytes 61472 | tf_op jit(solution)/shard_map/ppermute | solution.py:800
  112.2 1.2 collective-permute-done.19.p3
  113.5 0.6 assemble.1
  114.1 1.9 %collective-permute-start.20 = (f32[2,7680]{1,0:T(2,128)S(1)}, f32[2,7680]{1,0:T(2,128)S(1)}, u32[]{:S(2)}, u32[]{:S(2)}) collective-permute-start(f32[2,7680]{1,0:T(2,128)S(1)} %get-tuple-element.41), channel_id=1, source_target_pairs={{0,4},{4,8},{8,12},{12,16},{16,20},{20,24},{24,28},{28,32},{32,36}... | collective-permute-start | bytes 184328 | tf_op jit(solution)/shard_map/ppermute | solution.py:796
  116.0 18.6 %source_gradient.1.refs_4_ = f32[32,1536]{1,0:T(8,128)S(1)} custom-call(s32[32]{0:T(128)S(1)} %copy-done.3, bf16[32,1536]{1,0:T(8,128)(2,1)S(1)} %copy-done.1, f32[2,1536]{1,0:T(2,128)S(1)} %get-tuple-element.43.refs_1_, bf16[32,6144]{1,0:T(8,128)(2,1)S(1)} %get-tuple-element.26.yg_ref.refs_2_, f32[2,6144]{1,0:T(2,128)S(1)} %get-tuple-element.44.refs_3_), custom_call_target="tpu_custom_call" | custom-call | flops 4831838208 | bytes 4000000 | tf_op jit(solution)/shard_map/source_gradient/pallas_call | solution.py:777
  134.7 0.0 collective-permute-done.20.refs_1_.refs_3_
  134.7 8.2 %target_gradient.1 = f32[32,1536]{1,0:T(8,128)} custom-call(s32[32]{0:T(128)S(1)} %copy-done.3, bf16[32,1536]{1,0:T(8,128)(2,1)S(1)} %copy-done.1, f32[2,7680]{1,0:T(2,128)S(1)} %collective-permute-done.20.refs_1_.refs_3_, bf16[32,6144]{1,0:T(8,128)(2,1)S(1)} %collective-permute-done.13.refs_2_, f32[2,7680]{1,0:T(2,128)S(1)} %collective-permute-done.20.refs_1_.refs_3_, ...), custom_call_target="tpu_custom_call" | custom-call | flops 4831838208 | bytes 4000000 | tf_op jit(solution)/shard_map/target_gradient/pallas_call | solution.py:777
  (9 shorter events, 0.0 us)
Async XLA Ops:
  0.0 6.7 %collective-permute-start.3 = (bf16[32,1536]{1,0:T(8,128)(2,1)}, bf16[32,1536]{1,0:T(8,128)(2,1)S(1)}, u32[]{:S(2)}, u32[]{:S(2)}) collective-permute-start(bf16[32,1536]{1,0:T(8,128)(2,1)} %refs_0_.3), channel_id=1, source_target_pairs={{4,0},{8,4},{12,8},{16,12},{20,16},{24,20},{28,24},{32,28},{36,32}... | collective-permute-start | bytes 294920 | tf_op jit(solution)/shard_map/ppermute | solution.py:796
  3.0 8.8 %collective-permute-start.1 = (bf16[32,1536]{1,0:T(8,128)(2,1)}, bf16[32,1536]{1,0:T(8,128)(2,1)S(1)}, u32[]{:S(2)}, u32[]{:S(2)}) collective-permute-start(bf16[32,1536]{1,0:T(8,128)(2,1)} %refs_0_.3), channel_id=1, source_target_pairs={{0,2},{1,3},{2,0},{3,1},{4,6},{5,7},{6,4},{7,5},{8,10},{9,11},{10,... | collective-permute-start | bytes 294920 | tf_op jit(solution)/shard_map/ppermute | solution.py:800
  6.7 6.8 %collective-permute-start.5 = (bf16[32,1536]{1,0:T(8,128)(2,1)S(1)}, bf16[32,1536]{1,0:T(8,128)(2,1)S(1)}, u32[]{:S(2)}, u32[]{:S(2)}) collective-permute-start(bf16[32,1536]{1,0:T(8,128)(2,1)S(1)} %collective-permute-done.3.y0), channel_id=1, source_target_pairs={{0,2},{1,3},{2,0},{3,1},{4,6},{5,7},{6,4},{7,5},{8,10},{9,11},{10,... | collective-permute-start | bytes 294920 | tf_op jit(solution)/shard_map/ppermute | solution.py:800
  10.9 2.6 %collective-permute-start = (bf16[32,1536]{1,0:T(8,128)(2,1)}, bf16[32,1536]{1,0:T(8,128)(2,1)S(1)}, u32[]{:S(2)}, u32[]{:S(2)}) collective-permute-start(bf16[32,1536]{1,0:T(8,128)(2,1)} %refs_0_.3), channel_id=1, source_target_pairs={{0,1},{1,0},{2,3},{3,2},{4,5},{5,4},{6,7},{7,6},{8,9},{9,8},{10,11... | collective-permute-start | bytes 294920 | tf_op jit(solution)/shard_map/ppermute | solution.py:800
  10.9 2.6 %collective-permute-start.4 = (bf16[32,1536]{1,0:T(8,128)(2,1)S(1)}, bf16[32,1536]{1,0:T(8,128)(2,1)S(1)}, u32[]{:S(2)}, u32[]{:S(2)}) collective-permute-start(bf16[32,1536]{1,0:T(8,128)(2,1)S(1)} %collective-permute-done.3.y0), channel_id=1, source_target_pairs={{0,1},{1,0},{2,3},{3,2},{4,5},{5,4},{6,7},{7,6},{8,9},{9,8},{10,11... | collective-permute-start | bytes 294920 | tf_op jit(solution)/shard_map/ppermute | solution.py:800
  11.8 1.7 %collective-permute-start.2 = (bf16[32,1536]{1,0:T(8,128)(2,1)S(1)}, bf16[32,1536]{1,0:T(8,128)(2,1)S(1)}, u32[]{:S(2)}, u32[]{:S(2)}) collective-permute-start(bf16[32,1536]{1,0:T(8,128)(2,1)S(1)} %collective-permute-done.1.x2), channel_id=1, source_target_pairs={{0,1},{1,0},{2,3},{3,2},{4,5},{5,4},{6,7},{7,6},{8,9},{9,8},{10,11... | collective-permute-start | bytes 294920 | tf_op jit(solution)/shard_map/ppermute | solution.py:800
  13.5 1.3 collective-permute-start.6
  14.8 0.9 copy-start
  15.7 0.7 copy-start.2
  36.0 5.4 %collective-permute-start.8 = (f32[1,6144]{1,0:T(1,128)S(1)}, f32[1,6144]{1,0:T(1,128)S(1)}, u32[]{:S(2)}, u32[]{:S(2)}) collective-permute-start(f32[1,6144]{1,0:T(1,128)S(1)} %get-tuple-element.28.l0), channel_id=1, source_target_pairs={{0,2},{1,3},{2,0},{3,1},{4,6},{5,7},{6,4},{7,5},{8,10},{9,11},{10,... | collective-permute-start | bytes 73736 | tf_op jit(solution)/shard_map/ppermute | solution.py:800
  36.1 5.3 %collective-permute-start.7 = (f32[1,6144]{1,0:T(1,128)S(1)}, f32[1,6144]{1,0:T(1,128)S(1)}, u32[]{:S(2)}, u32[]{:S(2)}) collective-permute-start(f32[1,6144]{1,0:T(1,128)S(1)} %get-tuple-element.28.l0), channel_id=1, source_target_pairs={{0,1},{1,0},{2,3},{3,2},{4,5},{5,4},{6,7},{7,6},{8,9},{9,8},{10,11... | collective-permute-start | bytes 73736 | tf_op jit(solution)/shard_map/ppermute | solution.py:800
  41.4 1.2 collective-permute-start.9
  42.6 0.7 copy-start.3
  56.3 5.4 %collective-permute-start.11 = (f32[1,6144]{1,0:T(1,128)S(1)}, f32[1,6144]{1,0:T(1,128)S(1)}, u32[]{:S(2)}, u32[]{:S(2)}) collective-permute-start(f32[1,6144]{1,0:T(1,128)S(1)} %get-tuple-element.32.c0), channel_id=1, source_target_pairs={{0,2},{1,3},{2,0},{3,1},{4,6},{5,7},{6,4},{7,5},{8,10},{9,11},{10,... | collective-permute-start | bytes 73736 | tf_op jit(solution)/shard_map/ppermute | solution.py:800
  56.4 7.2 %collective-permute-start.10 = (f32[1,6144]{1,0:T(1,128)S(1)}, f32[1,6144]{1,0:T(1,128)S(1)}, u32[]{:S(2)}, u32[]{:S(2)}) collective-permute-start(f32[1,6144]{1,0:T(1,128)S(1)} %get-tuple-element.32.c0), channel_id=1, source_target_pairs={{0,1},{1,0},{2,3},{3,2},{4,5},{5,4},{6,7},{7,6},{8,9},{9,8},{10,11... | collective-permute-start | bytes 73736 | tf_op jit(solution)/shard_map/ppermute | solution.py:800
  61.7 1.9 %collective-permute-start.12 = (f32[1,6144]{1,0:T(1,128)S(1)}, f32[1,6144]{1,0:T(1,128)S(1)}, u32[]{:S(2)}, u32[]{:S(2)}) collective-permute-start(f32[1,6144]{1,0:T(1,128)S(1)} %collective-permute-done.11.c2), channel_id=1, source_target_pairs={{0,1},{1,0},{2,3},{3,2},{4,5},{5,4},{6,7},{7,6},{8,9},{9,8},{10,11... | collective-permute-start | bytes 73736 | tf_op jit(solution)/shard_map/ppermute | solution.py:800
  61.7 25.7 %collective-permute-start.13 = (bf16[32,6144]{1,0:T(8,128)(2,1)S(1)}, bf16[32,6144]{1,0:T(8,128)(2,1)S(1)}, u32[]{:S(2)}, u32[]{:S(2)}) collective-permute-start(bf16[32,6144]{1,0:T(8,128)(2,1)S(1)} %get-tuple-element.34), channel_id=1, source_target_pairs={{0,4},{4,8},{8,12},{12,16},{16,20},{20,24},{24,28},{28,32},{32,36}... | collective-permute-start | bytes 1179656 | tf_op jit(solution)/shard_map/ppermute | solution.py:796
  81.5 5.9 %collective-permute-start.15 = (f32[1,18432]{1,0:T(1,128)S(1)}, f32[1,18432]{1,0:T(1,128)S(1)}, u32[]{:S(2)}, u32[]{:S(2)}) collective-permute-start(f32[1,18432]{1,0:T(1,128)S(1)} %get-tuple-element.38.s0), channel_id=1, source_target_pairs={{0,2},{1,3},{2,0},{3,1},{4,6},{5,7},{6,4},{7,5},{8,10},{9,11},{10,... | collective-permute-start | bytes 221192 | tf_op jit(solution)/shard_map/ppermute | solution.py:800
  81.6 5.9 %collective-permute-start.14 = (f32[1,18432]{1,0:T(1,128)S(1)}, f32[1,18432]{1,0:T(1,128)S(1)}, u32[]{:S(2)}, u32[]{:S(2)}) collective-permute-start(f32[1,18432]{1,0:T(1,128)S(1)} %get-tuple-element.38.s0), channel_id=1, source_target_pairs={{0,1},{1,0},{2,3},{3,2},{4,5},{5,4},{6,7},{7,6},{8,9},{9,8},{10,11... | collective-permute-start | bytes 221192 | tf_op jit(solution)/shard_map/ppermute | solution.py:800
  87.5 1.3 collective-permute-start.16
  106.4 5.8 %collective-permute-start.18 = (f32[1,15360]{1,0:T(1,128)S(1)}, f32[1,15360]{1,0:T(1,128)S(1)}, u32[]{:S(2)}, u32[]{:S(2)}) collective-permute-start(f32[1,15360]{1,0:T(1,128)S(1)} %get-tuple-element.39.p0), channel_id=1, source_target_pairs={{0,2},{1,3},{2,0},{3,1},{4,6},{5,7},{6,4},{7,5},{8,10},{9,11},{10,... | collective-permute-start | bytes 184328 | tf_op jit(solution)/shard_map/ppermute | solution.py:800
  106.5 5.7 %collective-permute-start.17 = (f32[1,15360]{1,0:T(1,128)S(1)}, f32[1,15360]{1,0:T(1,128)S(1)}, u32[]{:S(2)}, u32[]{:S(2)}) collective-permute-start(f32[1,15360]{1,0:T(1,128)S(1)} %get-tuple-element.39.p0), channel_id=1, source_target_pairs={{0,1},{1,0},{2,3},{3,2},{4,5},{5,4},{6,7},{7,6},{8,9},{9,8},{10,11... | collective-permute-start | bytes 184328 | tf_op jit(solution)/shard_map/ppermute | solution.py:800
  112.2 1.2 collective-permute-start.19
  113.5 2.6 %copy-start.1 = (bf16[32,1536]{1,0:T(8,128)(2,1)S(1)}, bf16[32,1536]{1,0:T(8,128)(2,1)}, u32[]{:S(2)}) copy-start(bf16[32,1536]{1,0:T(8,128)(2,1)} %refs_0_.3) | copy-start | bytes 294916
  114.1 20.6 %collective-permute-start.20 = (f32[2,7680]{1,0:T(2,128)S(1)}, f32[2,7680]{1,0:T(2,128)S(1)}, u32[]{:S(2)}, u32[]{:S(2)}) collective-permute-start(f32[2,7680]{1,0:T(2,128)S(1)} %get-tuple-element.41), channel_id=1, source_target_pairs={{0,4},{4,8},{8,12},{12,16},{16,20},{20,24},{24,28},{28,32},{32,36}... | collective-permute-start | bytes 184328 | tf_op jit(solution)/shard_map/ppermute | solution.py:796
